TPU v7x, 256 devices: a whole 4x4x8 slice. The times are simulated.
256 devices in a mesh: nodes: 64 (over x, z, core), feat: 4 (over y).
Axes of the slice: x: 4, y: 4, z: 8, core: 2. Of those that a mesh axis runs over, the one named last changes fastest.
Arguments:
- features: bfloat16 [128, 262144], P('feat', 'nodes'), may hold values from -6 to 6
- w_self: bfloat16 [128, 256], replicated, may hold values from -0.5 to 0.5
- w_neigh: bfloat16 [128, 256], replicated, may hold values from -0.5 to 0.5
- hidden_bias: float32 [256], replicated, may hold values from -3 to 3
- cotangent: bfloat16 [256, 262144], P('feat', 'nodes'), may hold values from -0.01171875 to 0.01171875
- hub_local: int32 [64, 32], P('nodes'), may hold values from 0 to 4095
- send_rows: int32 [64, 64, 128], P('nodes'), may hold values from 0 to 4095
- send_count: int32 [64, 64], P('nodes'), may hold values from 0 to 128, as said below
- tile_values: bfloat16 [22528, 128, 128], P('nodes'), may hold values from 0 to 0.039794922
- tile_target: int32 [64, 352], P('nodes'), may hold values from 0 to 31, as said below
- tile_anchor: int32 [64, 352], P('nodes'), may hold values from 0 to 111, as said below
- tile_count: int32 [64], P('nodes'), may hold values from 112 to 352, as said below
Outputs:
- hidden: bfloat16 [256, 262144], P('feat', 'nodes')
- grad_self: float32 [128, 256], P(None, 'feat')
- grad_neigh: float32 [128, 256], P(None, 'feat')
- bias_grad: float32 [256], P('feat')
Inputs may be any that keep to these rules, and one draw needn't show every extreme that they name: hub_local[q, j] is the local row of partition q's j-th hub node; hubs are ordered by owner, then by j. send_rows[q, p, j] is the local row of partition q that fills slot j of what q sends to p; slots at or after send_count[q, p] are padding. `send_count`: A partition sends nothing to itself, and every partition fills all 128 slots for at least one other partition. `tile_target`: A block is 128 consecutive local nodes. On every partition each block is the destination of some live tile. `tile_anchor`: A block is 128 consecutive rows of source_p. On every partition each source block that holds halo or hub rows is used by some live tile. Tile slots at or after tile_count[p] are padding: their tile_values, tile_target and tile_anchor entries are arbitrary and must be ignored. Some partition fills all 352 slots.
All inputs are finite; a program needn't handle non-finite values.
Results may differ from a plain program's by a relative error of at most 0.0055.
Values may be sent and summed in bfloat16 or wider, within the bound.
A program may use at most 64 MiB of HBM per device.

v0:
```python
import jax
import jax.numpy as jnp
from jax import lax
from jax.sharding import PartitionSpec as P

TSTEP = 32


def local(
    features,
    w_self,
    w_neigh,
    hidden_bias,
    cotangent,
    hub_local,
    send_rows,
    send_count,
    tile_values,
    tile_target,
    tile_anchor,
    tile_count,
):
    node_parts = lax.axis_size("nodes")
    feat_parts = lax.axis_size("feat")
    feat_index = lax.axis_index("feat")
    width_local, node_local = features.shape
    slot_count = send_rows.shape[2]
    hub_count = hub_local.shape[1]
    tile_size = tile_values.shape[1]
    hidden_local = w_self.shape[1] // feat_parts
    own_hubs = jnp.take(features, hub_local[0], axis=1)
    outgoing = jnp.take(features, send_rows[0].reshape(-1), axis=1).reshape(
        width_local, node_parts, slot_count
    )
    live_slot = (
        lax.broadcasted_iota(jnp.int32, (node_parts, slot_count), 1) < send_count[0][:, None]
    )
    outgoing = jnp.where(live_slot[None], outgoing, jnp.zeros_like(outgoing))
    copies = jnp.broadcast_to(own_hubs[:, None, :], (width_local, node_parts, hub_count))
    halo_rows, hub_parts = (
        lax.all_to_all(outgoing, "nodes", split_axis=1, concat_axis=1, tiled=True),
        lax.all_to_all(copies, "nodes", split_axis=1, concat_axis=1, tiled=True),
    )
    hub_rows = hub_parts.reshape(width_local, node_parts * hub_count)
    source_rows = jnp.concatenate(
        [features, halo_rows.reshape(width_local, node_parts * slot_count), hub_rows], axis=1
    )
    source_blocks = source_rows.reshape(width_local, -1, tile_size)
    local_blocks = node_local // tile_size
    live_count = tile_count[0]
    turns = (live_count + TSTEP - 1) // TSTEP
    block_ids = jnp.arange(local_blocks, dtype=jnp.int32)

    def one_turn(turn_index, running):
        first_tile = turn_index * TSTEP
        tile_block = lax.dynamic_slice_in_dim(tile_values, first_tile, TSTEP, 0)
        targets = lax.dynamic_slice_in_dim(tile_target[0], first_tile, TSTEP, 0)
        anchors = lax.dynamic_slice_in_dim(tile_anchor[0], first_tile, TSTEP, 0)
        live_tiles = first_tile + jnp.arange(TSTEP, dtype=jnp.int32) < live_count
        picked = jnp.take(source_blocks, anchors, axis=1)
        products = jnp.einsum(
            "ftk,tik->fti", picked, tile_block, preferred_element_type=jnp.float32
        )
        selector = ((targets[:, None] == block_ids[None, :]) & live_tiles[:, None]).astype(
            jnp.float32
        )
        return running + jnp.einsum(
            "fti,tn->fni", products, selector, precision=lax.Precision.HIGHEST
        )

    empty = jnp.zeros((width_local, local_blocks, tile_size), jnp.float32)
    aggregate = (
        lax.fori_loop(0, turns, one_turn, empty)
        .reshape(width_local, node_local)
        .astype(jnp.bfloat16)
    )
    contract_first = (((0,), (0,)), ((), ()))
    contract_last = (((1,), (1,)), ((), ()))
    self_rows = lax.dynamic_slice_in_dim(w_self, feat_index * width_local, width_local, 0)
    neigh_rows = lax.dynamic_slice_in_dim(w_neigh, feat_index * width_local, width_local, 0)
    own_term = lax.dot_general(
        self_rows, features, contract_first, preferred_element_type=jnp.float32
    )
    preact = lax.psum_scatter(
        own_term
        + lax.dot_general(
            neigh_rows, aggregate, contract_first, preferred_element_type=jnp.float32
        ),
        "feat",
        scatter_dimension=0,
        tiled=True,
    )
    bias_local = lax.dynamic_slice_in_dim(hidden_bias, feat_index * hidden_local, hidden_local, 0)
    preact = preact + bias_local[:, None]
    sigmoid_value = jax.nn.sigmoid(preact)
    hidden = (preact * sigmoid_value).astype(jnp.bfloat16)
    pre_grad = (
        cotangent.astype(jnp.float32) * sigmoid_value * (1.0 + preact * (1.0 - sigmoid_value))
    ).astype(jnp.bfloat16)
    bias_part = jnp.sum(pre_grad, axis=1, dtype=jnp.float32)
    grad_piece = lax.all_gather(pre_grad, "feat", axis=0, tiled=True)
    own_grad = lax.dot_general(
        features, grad_piece, contract_last, preferred_element_type=jnp.float32
    )
    neigh_grad = lax.dot_general(
        aggregate, grad_piece, contract_last, preferred_element_type=jnp.float32
    )
    row_grads = jnp.stack([own_grad, neigh_grad])
    weight_part = lax.all_to_all(row_grads, "feat", split_axis=2, concat_axis=1, tiled=True)
    weight_total, bias_grad = lax.psum((weight_part, bias_part), "nodes")
    return (hidden, weight_total[0], weight_total[1], bias_grad)


def solution(mesh):
    in_specs = (
        P("feat", "nodes"),
        P(),
        P(),
        P(),
        P("feat", "nodes"),
        P("nodes", None),
        P("nodes", None, None),
        P("nodes", None),
        P("nodes", None, None),
        P("nodes", None),
        P("nodes", None),
        P("nodes"),
    )
    out_specs = (P("feat", "nodes"), P(None, "feat"), P(None, "feat"), P("feat"))
    return jax.shard_map(local, mesh=mesh, in_specs=in_specs, out_specs=out_specs, check_vma=False)
```

profile of v0, /device:TPU:1, one launch (start us, length us, event | category | flops | bytes accessed | tf_op | source)
XLA Modules:
  0.0 416.4 jit_solution(15025516311933367050)
XLA Ops:
  7.2 0.7 fusion.25
  7.9 0.7 compare_and_fusion.2
  8.6 1.4 copy.50
  10.0 0.6 gather_fusion.2
  10.8 1.1 reshape.199
  11.9 13.0 %all-to-all-start.1 = ((bf16[64,2,512]{2,1,0:T(2,128)(2,1)}), bf16[64,2,512]{2,1,0:T(2,128)(2,1)S(1)}, u32[]{:S(2)}, u32[]{:S(2)}) async-start(bf16[64,2,512]{2,1,0:T(2,128)(2,1)} %reshape.199), calls=%async_computation.1 | async-start | bytes 262144 | tf_op jit(solution)/shard_map/all_to_all | solution.py:42
  25.0 24.0 %gather_fusion.1 = bf16[8192,32]{1,0:T(8,128)(2,1)S(1)} fusion(bf16[32,4096]{0,1:T(8,128)(2,1)S(1)} %copy.50, s32[8192]{0:T(1024)S(1)} %broadcast_clamp_fusion), kind=kCustom, calls=%fused_computation.1 | custom fusion | bytes 1081344 | tf_op jit(solution)/shard_map/jit(_take)/gather | solution.py:32
  49.1 0.9 copy.51
  50.0 0.9 select_select_fusion
  50.9 10.3 %all-to-all-start = ((bf16[32,64,128]{2,0,1:T(8,128)(2,1)}), bf16[32,64,128]{2,0,1:T(8,128)(2,1)S(1)}, u32[]{:S(2)}, u32[]{:S(2)}) async-start(bf16[32,64,128]{2,0,1:T(8,128)(2,1)} %select_select_fusion), calls=%async_computation | async-start | bytes 1048576 | tf_op jit(solution)/shard_map/all_to_all | solution.py:41
  61.9 2.7 fusion.23
  65.7 12.8 %all-to-all-done = bf16[32,64,128]{2,0,1:T(8,128)(2,1)S(1)} async-done(((bf16[32,64,128]{2,0,1:T(8,128)(2,1)}), bf16[32,64,128]{2,0,1:T(8,128)(2,1)S(1)}, u32[]{:S(2)}, u32[]{:S(2)}) %all-to-all-start) | async-done | bytes 524320 | tf_op jit(solution)/shard_map/all_to_all | solution.py:41
  78.8 19.7 %while.11 = (s32[]{:T(128)}, f32[32,32,128]{2,1,0:T(8,128)S(1)}, s32[]{:T(128)}, s32[1,352]{1,0:T(1,128)}, s32[]{:T(128)}, /*index=5*/bf16[352,128,128]{2,1,0:T(...) while((s32[]{:T(128)}, f32[32,32,128]{2,1,0:T(8,128)S(1)}, ...), condition=%wide.region_1.2_spmd.clone, body=%wide.region_0.1_spmd.clone.sunk | while | flops 84151648 | bytes 3937595 | solution.py:73
  78.8 0.7 compare_and_fusion.4
  79.6 0.6 gather_fusion
  80.2 1.9 convolution_bitcast_fusion.5
  82.2 0.7 fusion.45
  82.9 0.8 fusion.46
  83.7 0.7 compare_and_fusion.4
  84.6 0.6 gather_fusion
  85.2 1.9 convolution_bitcast_fusion.5
  87.1 0.7 fusion.45
  87.8 0.8 fusion.46
  88.7 0.7 compare_and_fusion.4
  89.5 0.6 gather_fusion
  90.1 1.9 convolution_bitcast_fusion.5
  92.0 0.7 fusion.45
  92.7 0.8 fusion.46
  93.6 0.7 compare_and_fusion.4
  94.4 0.6 gather_fusion
  95.0 1.9 convolution_bitcast_fusion.5
  96.9 0.7 fusion.45
  97.7 0.8 fusion.46
  98.5 4.9 %convolution_add_fusion = f32[256,4096]{1,0:T(8,128)} fusion(f32[256,4096]{1,0:T(8,128)} %fusion.23, bf16[4,8,32,128]{3,2,1,0:T(8,128)(2,1)S(1)} %bitcast.96, bf16[128,256]{1,0:T(8,128)(2,1)} %param.16, s32[]{:T(128)S(6)} %select_n.87), kind=kOutput, calls=%fused_computation.29 | convolution fusion | flops 68157440 | bytes 8667140 | tf_op jit(solution)/shard_map/dot_general | solution.py:86
  103.5 0.6 copy-done.7
  104.2 79.5 %reduce-scatter.2.cloned.1.call-done = f32[64,4096]{1,0:T(8,128)} async-done(((f32[256,4096]{1,0:T(8,128)}), f32[64,4096]{1,0:T(8,128)}) %reduce-scatter.2.cloned.1.call-update) | async-done | bytes 1048592 | tf_op jit(solution)/shard_map/reduce_scatter | solution.py:84
  183.7 2.9 convert_reduce_fusion
  186.7 33.2 %all-gather.2.cloned.1.call-done = bf16[256,4096]{1,0:T(8,128)(2,1)} async-done(((bf16[64,4096]{1,0:T(8,128)(2,1)}), bf16[256,4096]{1,0:T(8,128)(2,1)}) %all-gather.2.cloned.1.call-update) | async-done | bytes 2097168 | tf_op jit(solution)/shard_map/all_gather | solution.py:101
  219.9 2.5 convolution_bitcast_fusion.2
  222.4 0.7 convolution_bitcast_fusion.3
  223.6 7.0 %all_to_all.28 = f32[4,1,4096]{2,1,0:T(1,128)S(1)} all-to-all(f32[4,1,4096]{2,1,0:T(1,128)S(1)} %reshape.201), channel_id=1, replica_groups=mesh['nodes'=64,'feat'=4] {'feat'}, dimensions={0} | all-to-all | bytes 131072 | tf_op jit(solution)/shard_map/all_to_all | solution.py:109
  231.1 0.8 reduce
  232.2 0.8 copy.58
  233.0 126.5 %psum.15 = f32[64]{0:T(128)} all-reduce(f32[64]{0:T(128)S(1)} %get-tuple-element.128), channel_id=1, replica_groups=mesh['nodes'=64,'feat'=4] {'nodes'}, use_global_device_ids=true, to_apply=%region_5.6 | all-reduce | flops 64 | bytes 512 | tf_op jit(solution)/shard_map/psum | solution.py:110
  359.5 48.0 %all-reduce.2.cloned.1.call-done = f32[2,128,64]{2,1,0:T(8,128)} async-done(((f32[2,128,64]{2,1,0:T(8,128)}), f32[2,128,64]{2,1,0:T(8,128)}) %all-reduce.2.cloned.1.call-update) | async-done | bytes 65552 | tf_op jit(solution)/shard_map/psum | solution.py:110
  407.6 0.9 slice_bitcast_fusion
  408.4 0.7 copy.59
  409.1 0.7 copy.60
  (50 shorter events, 3.5 us)
Async XLA Ops:
  7.2 54.8 %copy-start = (bf16[128,256]{1,0:T(8,128)(2,1)S(1)}, bf16[128,256]{1,0:T(8,128)(2,1)}, u32[]{:S(2)}) copy-start(bf16[128,256]{1,0:T(8,128)(2,1)} %param.15) | copy-start | bytes 196612
  7.2 17.7 %copy-start.4 = (s32[1,64,128]{2,1,0:T(8,128)S(1)}, s32[1,64,128]{2,1,0:T(8,128)}, u32[]{:S(2)}) copy-start(s32[1,64,128]{2,1,0:T(8,128)} %param.20) | copy-start | bytes 98308
  7.2 17.8 %copy-start.6 = (s32[1,64]{1,0:T(1,128)S(1)}, s32[1,64]{1,0:T(1,128)}, u32[]{:S(2)}) copy-start(s32[1,64]{1,0:T(1,128)} %param.21) | copy-start | bytes 772
  11.9 39.0 %all-to-all-start.1 = ((bf16[64,2,512]{2,1,0:T(2,128)(2,1)}), bf16[64,2,512]{2,1,0:T(2,128)(2,1)S(1)}, u32[]{:S(2)}, u32[]{:S(2)}) async-start(bf16[64,2,512]{2,1,0:T(2,128)(2,1)} %reshape.199), calls=%async_computation.1 | async-start | bytes 262144 | tf_op jit(solution)/shard_map/all_to_all | solution.py:42
  49.1 12.9 %copy-start.2 = (bf16[32,4096]{1,0:T(8,128)(2,1)S(1)}, bf16[32,4096]{1,0:T(8,128)(2,1)}, u32[]{:S(2)}) copy-start(bf16[32,4096]{1,0:T(8,128)(2,1)} %param.14) | copy-start | bytes 786436
  50.9 27.7 %all-to-all-start = ((bf16[32,64,128]{2,0,1:T(8,128)(2,1)}), bf16[32,64,128]{2,0,1:T(8,128)(2,1)S(1)}, u32[]{:S(2)}, u32[]{:S(2)}) async-start(bf16[32,64,128]{2,0,1:T(8,128)(2,1)} %select_select_fusion), calls=%async_computation | async-start | bytes 1048576 | tf_op jit(solution)/shard_map/all_to_all | solution.py:41
  61.2 122.5 %reduce-scatter.2.cloned.1.call-start = ((), (), s32[]{:S(2)}) async-start(), calls=%async_computation.4 | async-start | bytes 5242880 | tf_op jit(solution)/shard_map/reduce_scatter | solution.py:84
  65.1 13.7 %copy-start.5 = (s32[1,352]{1,0:T(1,128)S(1)}, s32[1,352]{1,0:T(1,128)}, u32[]{:S(2)}) copy-start(s32[1,352]{1,0:T(1,128)} %param.24) | copy-start | bytes 4228
  103.4 0.7 copy-start.7
  103.4 80.3 %copy-start.3 = (bf16[64,4096]{1,0:T(8,128)(2,1)S(1)}, bf16[64,4096]{1,0:T(8,128)(2,1)}, u32[]{:S(2)}) copy-start(bf16[64,4096]{1,0:T(8,128)(2,1)} %param.18) | copy-start | bytes 1572868
  103.5 116.4 %all-gather.2.cloned.1.call-start = ((), (), s32[]{:S(2)}) async-start(), calls=%async_computation.5 | async-start | bytes 2621440 | tf_op jit(solution)/shard_map/all_gather | solution.py:101
  186.7 220.9 %all-reduce.2.cloned.1.call-start = ((), (), s32[]{:S(2)}) async-start(), calls=%async_computation.6 | async-start | bytes 262144 | tf_op jit(solution)/shard_map/psum | solution.py:110
  219.9 2.5 copy-start.1
Sparse Core Ops, SparseCore 0:
  103.6 80.0 reduce-scatter.1
  186.8 33.0 all-gather.1
  233.1 174.3 all-reduce.1
where the time goes:
time: 417 us; the launch traced here: 416 us
  waiting for transfers between devices  174 us (42%)
  blocking collectives  134 us (32%)
  local copies, waits for them, and re-layouts  39.6 us (9%)
  starting transfers between devices  23.4 us (6%)
  matrix products  21.7 us (5%)
  between operations  14.7 us (4%)
  other arithmetic  9.63 us (2%)
    psum x1, blocking collectives, local(): weight_total, bias_grad = lax.psum((weight_part, bias_part), 'nodes')  127 us
    reduce_scatter x1, waiting for transfers between devices, local(): lax.psum_scatter(own_term + lax.dot_general(neigh_rows, aggregate, contra...  79.5 us
    psum x1, waiting for transfers between devices, local(): weight_total, bias_grad = lax.psum((weight_part, bias_part), 'nodes')  48 us
    all_gather x1, waiting for transfers between devices, local(): grad_piece = lax.all_gather(pre_grad, 'feat', axis=0, tiled=True)  33.2 us
    gather x2, local copies, waits for them, and re-layouts, local(): jnp.take(features, send_rows[0].reshape(-1), axis=1)  24.9 us
    all_to_all x1, starting transfers between devices, local(): lax.all_to_all(copies, 'nodes', split_axis=1, concat_axis=1, tiled=True)  13 us
    all_to_all x1, waiting for transfers between devices, local(): lax.all_to_all(outgoing, 'nodes', split_axis=1, concat_axis=1, tiled=True)  12.8 us
    all_to_all x1, starting transfers between devices, local(): lax.all_to_all(outgoing, 'nodes', split_axis=1, concat_axis=1, tiled=True)  10.3 us
  transfers between devices with their start and end apart: 5, of which 4 were waited for; matrix products, arithmetic and copies ran while one was open for 7% of the time, Pallas kernels for 0%

commit v1 on v0

v1 whole, which is shorter than its diff:
```python
import functools

import jax
import jax.numpy as jnp
from jax import lax
from jax.experimental import pallas as pl
from jax.experimental.pallas import tpu as pltpu
from jax.sharding import PartitionSpec as P

MESH = pl.DeviceIdType.MESH
NX, NZ, NN, NF = 4, 8, 64, 4
CHIPS = NX * NZ
VMEM = pl.BlockSpec(memory_space=pltpu.VMEM)
SMEM = pl.BlockSpec(memory_space=pltpu.SMEM)
TILES_STEP = 32
F32 = jnp.float32
BF16 = jnp.bfloat16


def greet(me, feat):
    barrier = pltpu.get_barrier_semaphore()

    def node(k, _):
        pl.semaphore_signal(
            barrier, inc=1, device_id={"nodes": (me + k) % NN, "feat": feat}, device_id_type=MESH
        )
        return 0

    lax.fori_loop(1, NN, node, 0)
    for k in range(1, NF):
        pl.semaphore_signal(
            barrier, inc=1, device_id={"nodes": me, "feat": (feat + k) % NF}, device_id_type=MESH
        )
    return barrier


def exchange_kernel(
    feat_ref, idx_ref, src_ref, full_ref, stacked, outbox, hub0, hub0_in, hub1, hub1_in,
    halo_send, halo_recv, feat_send, feat_recv, hub_send, hub_recv,
):
    me = lax.axis_index("nodes")
    feat = lax.axis_index("feat")
    core = me % 2
    z = (me // 2) % NZ
    x = me // (2 * NZ)
    barrier = greet(me, feat)

    for h in range(16):
        stacked[h * 32 : (h + 1) * 32, :] = feat_ref[:, h * 256 : (h + 1) * 256]

    def pick(row):
        index = idx_ref[pl.ds(row, 1), :]
        low = index & 255
        high = index >> 8
        hot = (lax.broadcasted_iota(jnp.int32, (256, 256), 0) == low).astype(F32).astype(BF16)
        parts = jnp.dot(stacked[...], hot, preferred_element_type=F32)
        out = jnp.zeros((32, 256), F32)
        for h in range(16):
            out = jnp.where(high == h, parts[h * 32 : (h + 1) * 32], out)
        return out.astype(BF16)

    hub0[...] = pick(CHIPS)[:, :128]
    pl.semaphore_wait(barrier, NN - 1 + NF - 1)

    def send(src, dst, send_sem, recv_sem, node, part):
        copy = pltpu.make_async_remote_copy(
            src_ref=src, dst_ref=dst, send_sem=send_sem, recv_sem=recv_sem,
            device_id={"nodes": node, "feat": part}, device_id_type=MESH,
        )
        copy.start()
        return copy

    sibling = me + 1 - 2 * core
    first = send(hub0, hub0_in, hub_send.at[0], hub_recv.at[0], sibling, feat)
    feat_copies = [
        send(feat_ref, full_ref.at[feat], feat_send.at[k], feat_recv.at[k], me, (feat + k) % NF)
        for k in range(1, NF)
    ]

    def halo_copy(node):
        return pltpu.make_async_remote_copy(
            src_ref=outbox.at[node], dst_ref=src_ref.at[32 + me],
            send_sem=halo_send.at[node], recv_sem=halo_recv.at[me],
            device_id={"nodes": node, "feat": feat}, device_id_type=MESH,
        )

    def step(i, _):
        turn = i % NZ
        dx = i // NZ
        dz = (4 + (1 - 2 * (turn % 2)) * ((turn + 1) // 2)) % NZ
        chip = ((x + dx) % NX) * NZ + (z + dz) % NZ
        rows = pick(chip)
        outbox[2 * chip] = rows[:, :128]
        outbox[2 * chip + 1] = rows[:, 128:]
        halo_copy(2 * chip).start()
        halo_copy(2 * chip + 1).start()
        return 0

    def own_chip():
        chip = me // 2
        rows = pick(chip)
        outbox[2 * chip] = rows[:, :128]
        outbox[2 * chip + 1] = rows[:, 128:]
        halo_copy(sibling).start()
        src_ref[32 + me] = jnp.zeros((32, 128), BF16)

    own_chip()
    lax.fori_loop(0, 3, step, 0)
    first.wait()
    hub1[...] = hub0[...] + hub0_in[...]
    across = x * 2 * NZ + (z + 1 - 2 * (z % 2)) * 2 + core
    second = send(hub1, hub1_in, hub_send.at[1], hub_recv.at[1], across, feat)
    lax.fori_loop(3, 7, step, 0)
    second.wait()
    block = 96 + me // 4
    src_ref[block] = hub1[...] + hub1_in[...]
    along_z = [
        send(
            src_ref.at[block], src_ref.at[block], hub_send.at[1 + k], hub_recv.at[1 + k],
            x * 2 * NZ + ((z + 2 * k) % NZ) * 2 + core, feat,
        )
        for k in range(1, 4)
    ]
    lax.fori_loop(8, 18, step, 0)
    for copy in along_z:
        copy.wait()
    group = src_ref.at[pl.ds(96 + x * 4, 4)]
    along_x = [
        send(
            group, group, hub_send.at[4 + k], hub_recv.at[4 + k],
            ((x + k) % NX) * 2 * NZ + z * 2 + core, feat,
        )
        for k in range(1, 4)
    ]
    lax.fori_loop(18, 32, step, 0)
    for b in range(32):
        src_ref[b] = feat_ref[:, b * 128 : (b + 1) * 128]
    full_ref[feat] = feat_ref[...]
    for copy in along_x:
        copy.wait()
    for copy in feat_copies:
        copy.wait()

    def arrived(k, _):
        node = (me + k) % NN
        pltpu.make_async_remote_copy(
            src_ref=outbox.at[node], dst_ref=src_ref.at[32 + node],
            send_sem=halo_send.at[node], recv_sem=halo_recv.at[node],
            device_id={"nodes": node, "feat": feat}, device_id_type=MESH,
        ).wait()
        return 0

    lax.fori_loop(1, NN, arrived, 0)


def exchange(features, index):
    cols = features.shape[1]
    return pl.pallas_call(
        exchange_kernel,
        name="exchange",
        out_shape=(
            jax.ShapeDtypeStruct((112, 32, 128), BF16),
            jax.ShapeDtypeStruct((NF, 32, cols), BF16),
        ),
        in_specs=[VMEM, VMEM],
        out_specs=(VMEM, VMEM),
        scratch_shapes=[
            pltpu.VMEM((512, 256), BF16),
            pltpu.VMEM((NN, 32, 128), BF16),
            pltpu.VMEM((32, 128), BF16),
            pltpu.VMEM((32, 128), BF16),
            pltpu.VMEM((32, 128), BF16),
            pltpu.VMEM((32, 128), BF16),
            pltpu.SemaphoreType.DMA((NN,)),
            pltpu.SemaphoreType.DMA((NN,)),
            pltpu.SemaphoreType.DMA((NF,)),
            pltpu.SemaphoreType.DMA((NF,)),
            pltpu.SemaphoreType.DMA((8,)),
            pltpu.SemaphoreType.DMA((8,)),
        ],
        compiler_params=pltpu.CompilerParams(
            collective_id=0, has_side_effects=True, vmem_limit_bytes=32 * 2**20
        ),
    )(features, index)


def tiles_kernel(count, targets, anchors, values_ref, src_ref, out_ref, sums):
    turn = pl.program_id(0)
    lanes = sums.shape[0]

    @pl.when(turn == 0)
    def _():
        sums[...] = jnp.zeros_like(sums)

    live = count[0]

    def batch(b, _):
        first = b * 16
        products = []
        spots = []
        for j in range(16):
            slot = turn * TILES_STEP + first + j
            block = jnp.clip(anchors[0, slot], 0, 111)
            product = lax.dot_general(
                src_ref[block], values_ref[first + j], (((1,), (1,)), ((), ())),
                preferred_element_type=F32,
            )
            products.append(jnp.where(slot < live, product, 0.0))
            spots.append(jnp.clip(targets[0, slot], 0, 31))
        for j in range(16):
            sums[j % lanes, spots[j]] += products[j]
        return 0

    lax.fori_loop(0, TILES_STEP // 16, batch, 0)

    @pl.when(turn == pl.num_programs(0) - 1)
    def _():
        for d in range(32):
            total = sums[0, d]
            for lane in range(1, lanes):
                total = total + sums[lane, d]
            out_ref[:, d * 128 : (d + 1) * 128] = total.astype(BF16)


def tile_sums(count, targets, anchors, values, source):
    steps = values.shape[0] // TILES_STEP
    return pl.pallas_call(
        tiles_kernel,
        name="tile_sums",
        grid_spec=pltpu.PrefetchScalarGridSpec(
            num_scalar_prefetch=3,
            grid=(steps,),
            in_specs=[
                pl.BlockSpec((TILES_STEP, 128, 128), lambda i, *_: (i, 0, 0)),
                VMEM,
            ],
            out_specs=pl.BlockSpec((32, 4096), lambda i, *_: (0, 0)),
            scratch_shapes=[pltpu.VMEM((4, 32, 32, 128), F32)],
        ),
        out_shape=jax.ShapeDtypeStruct((32, 4096), BF16),
        compiler_params=pltpu.CompilerParams(vmem_limit_bytes=32 * 2**20),
    )(count, targets, anchors, values, source)


def layer_kernel(
    agg_ref, full_ref, wself_ref, wneigh_ref, bias_ref, cot_ref,
    hidden_ref, gself_ref, gneigh_ref, gbias_ref,
    aggs, weights, bias, sums, pieces, inbox, totals,
    agg_send, agg_recv, piece_send, piece_recv, total_send, total_recv,
):
    me = lax.axis_index("nodes")
    feat = lax.axis_index("feat")
    barrier = greet(me, feat)

    def mine(ref):
        part = ref[:, 0:64]
        for k in range(1, NF):
            part = jnp.where(feat == k, ref[:, k * 64 : (k + 1) * 64], part)
        return part

    weights[0] = mine(wself_ref).T
    weights[1] = mine(wneigh_ref).T
    bias[...] = jnp.broadcast_to(mine(bias_ref), (128, 64)).T
    aggs[feat] = agg_ref[...]
    sums[...] = jnp.zeros_like(sums)
    pieces[16] = jnp.zeros((8, 128), F32)
    pl.semaphore_wait(barrier, NN - 1 + NF - 1)

    copies = []
    for k in range(1, NF):
        copy = pltpu.make_async_remote_copy(
            src_ref=agg_ref, dst_ref=aggs.at[feat],
            send_sem=agg_send.at[k], recv_sem=agg_recv.at[k],
            device_id={"nodes": me, "feat": (feat + k) % NF}, device_id_type=MESH,
        )
        copy.start()
        copies.append(copy)
    for copy in copies:
        copy.wait()

    last = (((1,), (1,)), ((), ()))
    width = 512

    def columns(c, _):
        span = pl.ds(pl.multiple_of(c * width, width), width)
        own = full_ref[:, :, span].reshape(128, width)
        neigh = aggs[:, :, span].reshape(128, width)
        pre = jnp.dot(weights[0], own, preferred_element_type=F32)
        pre = pre + jnp.dot(weights[1], neigh, preferred_element_type=F32)
        pre = pre + bias[:, 0:1]
        gate = jax.nn.sigmoid(pre)
        hidden_ref[:, span] = (pre * gate).astype(BF16)
        grad = (cot_ref[:, span].astype(F32) * gate * (1.0 + pre * (1.0 - gate))).astype(BF16)
        sums[0:128, :] += lax.dot_general(own, grad, last, preferred_element_type=F32)
        sums[128:256, :] += lax.dot_general(neigh, grad, last, preferred_element_type=F32)
        sums[256:264, :] += lax.dot_general(
            jnp.ones((8, width), BF16), grad, last, preferred_element_type=F32
        )
        return 0

    lax.fori_loop(0, cot_ref.shape[1] // width, columns, 0)

    for r in range(16):
        pieces[r] = jnp.concatenate(
            [sums[8 * r : 8 * r + 8, :], sums[128 + 8 * r : 136 + 8 * r, :]], axis=1
        )
    pieces[16, :, 0:64] = sums[256:264, :]

    def piece_copy(r):
        return pltpu.make_async_remote_copy(
            src_ref=pieces.at[r], dst_ref=inbox.at[me],
            send_sem=piece_send.at[r], recv_sem=piece_recv.at[me],
            device_id={"nodes": 3 * r, "feat": feat}, device_id_type=MESH,
        )

    def total_copy(r, node):
        return pltpu.make_async_remote_copy(
            src_ref=totals.at[r], dst_ref=totals.at[r],
            send_sem=total_send.at[node], recv_sem=total_recv.at[r],
            device_id={"nodes": node, "feat": feat}, device_id_type=MESH,
        )

    for r in range(17):

        @pl.when(me != 3 * r)
        def _():
            piece_copy(r).start()

    reducer = jnp.logical_and(me % 3 == 0, me <= 48)

    @pl.when(reducer)
    def _():
        r = me // 3
        inbox[me] = pieces[r]

        def arrived(k, _):
            node = (me + k) % NN
            pltpu.make_async_remote_copy(
                src_ref=pieces.at[r], dst_ref=inbox.at[node],
                send_sem=piece_send.at[r], recv_sem=piece_recv.at[node],
                device_id={"nodes": node, "feat": feat}, device_id_type=MESH,
            ).wait_recv()
            return 0

        lax.fori_loop(1, NN, arrived, 0)
        totals[r] = jnp.sum(inbox[...], axis=0)

        def give(k, _):
            total_copy(r, (me + k) % NN).start()
            return 0

        lax.fori_loop(1, NN, give, 0)

        def given(k, _):
            total_copy(r, (me + k) % NN).wait_send()
            return 0

        lax.fori_loop(1, NN, given, 0)

    for r in range(17):

        @pl.when(me != 3 * r)
        def _():
            piece_copy(r).wait_send()
            total_copy(r, 3 * r).wait_recv()

    for r in range(16):
        gself_ref[8 * r : 8 * r + 8, :] = totals[r, :, 0:64]
        gneigh_ref[8 * r : 8 * r + 8, :] = totals[r, :, 64:128]
    gbias_ref[...] = totals[16, 0:1, 0:64]


def layer(agg, full, w_self, w_neigh, bias, cotangent):
    cols = cotangent.shape[1]
    return pl.pallas_call(
        layer_kernel,
        name="layer",
        out_shape=(
            jax.ShapeDtypeStruct((64, cols), BF16),
            jax.ShapeDtypeStruct((128, 64), F32),
            jax.ShapeDtypeStruct((128, 64), F32),
            jax.ShapeDtypeStruct((1, 64), F32),
        ),
        in_specs=[VMEM] * 6,
        out_specs=(VMEM,) * 4,
        scratch_shapes=[
            pltpu.VMEM((NF, 32, cols), BF16),
            pltpu.VMEM((2, 64, 128), BF16),
            pltpu.VMEM((64, 128), F32),
            pltpu.VMEM((264, 64), F32),
            pltpu.VMEM((17, 8, 128), F32),
            pltpu.VMEM((NN, 8, 128), F32),
            pltpu.VMEM((17, 8, 128), F32),
            pltpu.SemaphoreType.DMA((NF,)),
            pltpu.SemaphoreType.DMA((NF,)),
            pltpu.SemaphoreType.DMA((17,)),
            pltpu.SemaphoreType.DMA((NN,)),
            pltpu.SemaphoreType.DMA((NN,)),
            pltpu.SemaphoreType.DMA((17,)),
        ],
        compiler_params=pltpu.CompilerParams(
            collective_id=1, has_side_effects=True, vmem_limit_bytes=32 * 2**20
        ),
    )(agg, full, w_self, w_neigh, bias, cotangent)


def local(
    features, w_self, w_neigh, hidden_bias, cotangent, hub_local, send_rows, send_count,
    tile_values, tile_target, tile_anchor, tile_count,
):
    me = lax.axis_index("nodes")
    slots = lax.broadcasted_iota(jnp.int32, (NN, 128), 1)
    rows = jnp.where(slots < send_count[0][:, None], send_rows[0], -1).reshape(CHIPS, 256)
    lane = lax.broadcasted_iota(jnp.int32, (1, 256), 1)
    hubs = jnp.where(lane // 32 == me % 4, jnp.tile(hub_local, (1, 8)), -1)
    index = jnp.concatenate([rows, hubs], axis=0)
    source, full = exchange(features, index)
    agg = tile_sums(tile_count, tile_target, tile_anchor, tile_values, source)
    hidden, grad_self, grad_neigh, bias_grad = layer(
        agg, full, w_self, w_neigh, hidden_bias.reshape(1, -1), cotangent
    )
    return hidden, grad_self, grad_neigh, bias_grad.reshape(-1)


def solution(mesh):
    in_specs = (
        P("feat", "nodes"), P(), P(), P(), P("feat", "nodes"), P("nodes", None),
        P("nodes", None, None), P("nodes", None), P("nodes", None, None), P("nodes", None),
        P("nodes", None), P("nodes"),
    )
    out_specs = (P("feat", "nodes"), P(None, "feat"), P(None, "feat"), P("feat"))
    return jax.shard_map(local, mesh=mesh, in_specs=in_specs, out_specs=out_specs, check_vma=False)
```

time: 417 us -> 93.1 us (0.22)
  waiting for transfers between devices: 174 us -> 0 us
  blocking collectives: 134 us -> 0 us
  Pallas kernels: 0 us -> 78.5 us
  local copies, waits for them, and re-layouts: 39.6 us -> 11.5 us
  starting transfers between devices: 23.4 us -> 0 us
  matrix products: 21.7 us -> 0 us
  between operations: 14.7 us -> 1.47 us
  other arithmetic: 9.63 us -> 1.34 us
    psum x1 -> x0, blocking collectives: 127 us -> none  [local(): weight_total, bias_grad = lax.psum((weight_part, bias_part), 'nodes')]
    reduce_scatter x1 -> x0, waiting for transfers between devices: 79.5 us -> none  [local(): lax.psum_scatter(own_term + lax.dot_general(neigh_rows, aggregate, contra...]
    pallas_call x0 -> x3, Pallas kernels: none -> 78.5 us  [the longest x1 39.4 us: layer(): pl.pallas_call(layer_kernel, name='layer', out_shape=(jax.ShapeDtypeStruc...]
    psum x1 -> x0, waiting for transfers between devices: 48 us -> none  [local(): weight_total, bias_grad = lax.psum((weight_part, bias_part), 'nodes')]
    all_gather x1 -> x0, waiting for transfers between devices: 33.2 us -> none  [local(): grad_piece = lax.all_gather(pre_grad, 'feat', axis=0, tiled=True)]
    gather x7 -> x0, local copies, waits for them, and re-layouts: 27.9 us -> none  [the longest x2 24.9 us: local(): jnp.take(features, send_rows[0].reshape(-1), axis=1)]
    all_to_all x2 -> x0, starting transfers between devices: 23.3 us -> none  [the longest x1 13 us: local(): lax.all_to_all(copies, 'nodes', split_axis=1, concat_axis=1, tiled=True)]
    dot_general x12 -> x0, matrix products: 21.7 us -> none  [the longest x4 7.66 us: one_turn(): jnp.einsum('ftk,tik->fti', picked, tile_block, preferred_element_type=jnp...]
  transfers between devices with their start and end apart: 5 -> 0, of which waited for: 4 -> 0; matrix products, arithmetic and copies ran while one was open for 7% -> 0% of each run, Pallas kernels for 0% -> 0%
where the time goes in v1:
time: 93.1 us; the launch traced here: 92.8 us
  Pallas kernels  78.5 us (84%)
  local copies, waits for them, and re-layouts  11.5 us (12%)
  between operations  1.47 us (2%)
  other arithmetic  1.34 us (1%)
    pallas_call x1, Pallas kernels, layer(): pl.pallas_call(layer_kernel, name='layer', out_shape=(jax.ShapeDtypeStruc...  39.4 us
    pallas_call x1, Pallas kernels, exchange(): pl.pallas_call(exchange_kernel, name='exchange', out_shape=(jax.ShapeDtyp...  29.6 us
    unnamed x21, local copies, waits for them, and re-layouts  9.8 us
    pallas_call x1, Pallas kernels, tile_sums(): pl.pallas_call(tiles_kernel, name='tile_sums', grid_spec=pltpu.PrefetchSc...  9.46 us

profile of v1, /device:TPU:1, one launch (start us, length us, event | category | flops | bytes accessed | tf_op | source)
XLA Modules:
  0.0 92.8 jit_solution(13822799159205810440)
XLA Ops:
  0.6 0.0 copy-start.1
  1.4 0.5 broadcast.79
  1.9 1.3 %reduce.3 = s32[64]{0:T(128)S(1)} reduce(s32[1,64]{1,0:T(1,128)} %param.19, s32[]{:T(128)} %broadcast.79), dimensions={0}, to_apply=%param.19.reduce_sub_computation.3 | reduce | bytes 516 | tf_op args[7]
  3.2 0.7 tile.12
  3.8 0.1 tile.13
  3.9 0.1 lt.19
  4.0 0.1 lt.20
  4.1 0.8 squeeze.3
  4.9 0.0 copy-start.2
  5.0 0.9 %copy-done.2 = bf16[32,4096]{1,0:T(8,128)(2,1)S(1)} copy-done((bf16[32,4096]{1,0:T(8,128)(2,1)S(1)}, bf16[32,4096]{1,0:T(8,128)(2,1)}, u32[]{:S(2)}) %copy-start.2) | copy-done | bytes 262168
  5.9 0.0 copy-start.3
  5.9 0.0 copy-start.4
  5.9 0.0 copy-start.7
  5.9 29.6 %exchange.1 = (bf16[112,32,128]{2,1,0:T(8,128)(2,1)S(1)}, bf16[4,32,4096]{2,1,0:T(8,128)(2,1)S(1)}) custom-call(bf16[32,4096]{1,0:T(8,128)(2,1)S(1)} %copy-done.2, s32[33,256]{1,0:T(8,128)S(1)} %pad_add_fusion.idx_ref), custom_call_target="tpu_custom_call" | custom-call | tf_op jit(solution)/shard_map/exchange/pallas_call | solution.py:158
  35.5 0.0 copy-start
  35.5 4.3 %copy-done = bf16[352,128,128]{2,1,0:T(8,128)(2,1)S(1)} copy-done((bf16[352,128,128]{2,1,0:T(8,128)(2,1)S(1)}, bf16[352,128,128]{2,1,0:T(8,128)(2,1)}, u32[]{:S(2)}) %copy-start) | copy-done | bytes 11534360
  39.8 0.0 copy-start.5
  39.8 0.7 copy-done.5
  40.5 0.0 copy-start.6
  40.5 0.7 copy-done.6
  41.2 9.5 %tile_sums.1.agg_ref = bf16[32,4096]{1,0:T(8,128)(2,1)S(1)} custom-call(s32[1]{0:T(128)S(6)} %copy.26.count, s32[1,352]{1,0:T(1,128)S(1)} %copy-done.5, s32[1,352]{1,0:T(1,128)S(1)} %copy-done.6, bf16[352,128,128]{2,1,0:T(8,128)(2,1)S(1)} %copy-done, bf16[112,32,128]{2,1,0:T(8,128)(2,1)S(1)} %get-tuple-element.10.src_ref), custom_call_target="tpu_custom_call" | custom-call | tf_op jit(solution)/shard_map/tile_sums/pallas_call | solution.py:227
  50.6 0.0 copy-done.1
  50.6 0.0 copy-done.3
  50.6 0.0 copy-done.4
  50.7 0.0 copy-done.7
  50.7 39.4 %layer.1 = (bf16[64,4096]{1,0:T(8,128)(2,1)S(1)}, f32[128,64]{1,0:T(8,128)S(1)}, f32[128,64]{1,0:T(8,128)S(1)}, f32[1,64]{1,0:T(1,128)S(1)}) custom-call(bf16[32,4096]{1,0:T(8,128)(2,1)S(1)} %tile_sums.1.agg_ref, bf16[4,32,4096]{2,1,0:T(8,128)(2,1)S(1)} %get-tuple-element.11.full_ref, bf16[128,256]{1,0:T(8,128)(2,1)S(1)} %copy-done.3, ...), custom_call_target="tpu_custom_call" | custom-call | tf_op jit(solution)/shard_map/layer/pallas_call | solution.py:375
  90.1 0.7 copy.18
  90.8 0.7 copy.19
  91.5 0.8 copy.27
  92.3 0.5 copy.28
  (4 shorter events, 0.0 us)
Async XLA Ops:
  0.6 50.0 %copy-start.1 = (bf16[64,4096]{1,0:T(8,128)(2,1)S(1)}, bf16[64,4096]{1,0:T(8,128)(2,1)}, u32[]{:S(2)}) copy-start(bf16[64,4096]{1,0:T(8,128)(2,1)} %cot_ref.1) | copy-start | bytes 1572868
  4.9 1.0 %copy-start.2 = (bf16[32,4096]{1,0:T(8,128)(2,1)S(1)}, bf16[32,4096]{1,0:T(8,128)(2,1)}, u32[]{:S(2)}) copy-start(bf16[32,4096]{1,0:T(8,128)(2,1)} %feat_ref.1) | copy-start | bytes 786436
  5.9 44.7 %copy-start.3 = (bf16[128,256]{1,0:T(8,128)(2,1)S(1)}, bf16[128,256]{1,0:T(8,128)(2,1)}, u32[]{:S(2)}) copy-start(bf16[128,256]{1,0:T(8,128)(2,1)} %wself_ref.1) | copy-start | bytes 196612
  5.9 44.7 %copy-start.4 = (bf16[128,256]{1,0:T(8,128)(2,1)S(1)}, bf16[128,256]{1,0:T(8,128)(2,1)}, u32[]{:S(2)}) copy-start(bf16[128,256]{1,0:T(8,128)(2,1)} %wneigh_ref.1) | copy-start | bytes 196612
  5.9 44.8 %copy-start.7 = (f32[256]{0:T(256)S(1)}, f32[256]{0:T(256)}, u32[]{:S(2)}) copy-start(f32[256]{0:T(256)} %param.15) | copy-start | bytes 3076
  35.5 4.3 %copy-start = (bf16[352,128,128]{2,1,0:T(8,128)(2,1)S(1)}, bf16[352,128,128]{2,1,0:T(8,128)(2,1)}, u32[]{:S(2)}) copy-start(bf16[352,128,128]{2,1,0:T(8,128)(2,1)} %values_ref.1) | copy-start | bytes 34603012
  39.8 0.7 copy-start.5
  40.5 0.7 copy-start.6

commit v2 on v0

v2 whole, which is shorter than its diff:
```python
import jax
import jax.numpy as jnp
from jax import lax
from jax.experimental import pallas as pl
from jax.experimental.pallas import tpu as pltpu
from jax.sharding import PartitionSpec as P

MESH = pl.DeviceIdType.MESH
NX, NZ, NN, NF = 4, 8, 64, 4
TILES = 352
BLOCKS = 32
UNROLL = 32
PARTS = 8
LAST = (((1,), (1,)), ((), ()))
F32 = jnp.float32
BF16 = jnp.bfloat16
I32 = jnp.int32


def peer_signal(barrier, node, part):
    pl.semaphore_signal(
        barrier, inc=1, device_id={"nodes": node, "feat": part}, device_id_type=MESH
    )


def remote(src, dst, send_sem, recv_sem, node, part):
    return pltpu.make_async_remote_copy(
        src_ref=src, dst_ref=dst, send_sem=send_sem, recv_sem=recv_sem,
        device_id={"nodes": node, "feat": part}, device_id_type=MESH,
    )


def started(copy):
    copy.start()
    return copy


def layer_kernel(
    feat_in, wself_in, wneigh_in, bias_in, cot_in, hub_in, rows_in, count_in, values_in, target_in,
    anchor_in, live_in, hidden_ref, gself_ref, gneigh_ref, gbias_ref,
    feat_ref, wself_ref, wneigh_ref, bias_ref, cot_ref, hub_ref, rows_ref, count_ref, values_ref,
    target_ref, anchor_ref, live_ref,
    src_ref, full_ref, stacked, outbox, hub0, hub0_in, hub1, hub1_in, table, order, running,
    aggs, weights, bias, own_term, sums, pieces, inbox, partial, crossbox, totals,
    load_sem, table_sem, halo_send, halo_recv, feat_send, feat_recv, hub_send, hub_recv,
    agg_send, agg_recv, reduce_send, reduce_recv,
):
    me = lax.axis_index("nodes")
    feat = lax.axis_index("feat")
    core = me % 2
    z = (me // 2) % NZ
    x = me // (2 * NZ)
    loads = [
        started(pltpu.make_async_copy(src, dst, load_sem.at[i]))
        for i, (src, dst) in enumerate(
            (
                (feat_in, feat_ref), (rows_in, rows_ref), (hub_in, hub_ref), (count_in, count_ref),
                (target_in, target_ref), (anchor_in, anchor_ref), (live_in, live_ref),
                (wself_in, wself_ref), (wneigh_in, wneigh_ref), (bias_in, bias_ref),
                (cot_in, cot_ref), (values_in, values_ref),
            )
        )
    ]
    barrier = pltpu.get_barrier_semaphore()

    def node_signal(k, _):
        peer_signal(barrier, (me + k) % NN, feat)
        return 0

    lax.fori_loop(1, NN, node_signal, 0)
    for k in range(1, NF):
        peer_signal(barrier, me, (feat + k) % NF)

    for copy in loads[:4]:
        copy.wait()
    for h in range(16):
        stacked[h * 32 : (h + 1) * 32, :] = feat_ref[:, h * 256 : (h + 1) * 256]
    lane = lax.broadcasted_iota(I32, (1, 128), 1)

    def pick(index):
        low = index & 255
        high = index >> 8
        hot = (lax.broadcasted_iota(I32, (256, 256), 0) == low).astype(F32).astype(BF16)
        parts = jnp.dot(stacked[...], hot, preferred_element_type=F32)
        out = jnp.zeros((32, 256), F32)
        for h in range(16):
            out = jnp.where(high == h, parts[h * 32 : (h + 1) * 32], out)
        return out.astype(BF16)

    def fill(chip):
        first = jnp.where(lane < count_ref[0, 2 * chip], rows_ref[pl.ds(2 * chip, 1), :], -1)
        second = jnp.where(
            lane < count_ref[0, 2 * chip + 1], rows_ref[pl.ds(2 * chip + 1, 1), :], -1
        )
        rows = pick(jnp.concatenate([first, second], axis=1))
        outbox[2 * chip] = rows[:, :128]
        outbox[2 * chip + 1] = rows[:, 128:]

    def halo_copy(node):
        return remote(
            outbox.at[node], src_ref.at[32 + me], halo_send.at[node], halo_recv.at[me], node, feat
        )

    def chip_at(k, dz):
        dx = 2 + (1 - 2 * (k % 2)) * ((k + 1) // 2)
        return ((x + dx) % NX) * NZ + (z + dz) % NZ

    def send(chip):
        halo_copy(2 * chip).start()
        halo_copy(2 * chip + 1).start()

    def opposite(k, _):
        fill(chip_at(k, 4))
        return 0

    def opposite_send(k, _):
        send(chip_at(k, 4))
        return 0

    def between(j, _):
        turn = j % 8
        dz = 4 + (2 * (turn % 2) - 1) * (1 + j // 8)
        chip = chip_at(turn // 2, dz)
        fill(chip)
        send(chip)
        return 0

    def level(k, _):
        chip = chip_at(k, 0)
        fill(chip)
        send(chip)
        return 0

    sibling = me + 1 - 2 * core
    hubs = jnp.concatenate([hub_ref[...]] * 4, axis=1)
    hubs = jnp.where(lane // 32 == me % 4, hubs, -1)
    hub0[...] = pick(jnp.concatenate([hubs, jnp.full_like(hubs, -1)], axis=1))[:, :128]
    src_ref[32 + me] = jnp.zeros((32, 128), BF16)
    lax.fori_loop(0, 4, opposite, 0)
    pl.semaphore_wait(barrier, NN - 1 + NF - 1)

    first = started(remote(hub0, hub0_in, hub_send.at[0], hub_recv.at[0], sibling, feat))
    feat_copies = [
        started(
            remote(
                feat_ref, full_ref.at[feat], feat_send.at[k], feat_recv.at[k], me,
                (feat + k) % NF,
            )
        )
        for k in range(1, NF)
    ]
    lax.fori_loop(0, 4, opposite_send, 0)
    lax.fori_loop(0, 2, between, 0)
    first.wait()
    hub1[...] = hub0[...] + hub0_in[...]
    across_pair = x * 2 * NZ + (z + 1 - 2 * (z % 2)) * 2 + core
    second = started(remote(hub1, hub1_in, hub_send.at[1], hub_recv.at[1], across_pair, feat))
    lax.fori_loop(2, 9, between, 0)
    second.wait()
    block = 96 + me // 4
    src_ref[block] = hub1[...] + hub1_in[...]
    along_z = [
        started(
            remote(
                src_ref.at[block], src_ref.at[block], hub_send.at[1 + k], hub_recv.at[1 + k],
                x * 2 * NZ + ((z + 2 * k) % NZ) * 2 + core, feat,
            )
        )
        for k in range(1, 4)
    ]
    lax.fori_loop(9, 22, between, 0)
    for copy in along_z:
        copy.wait()
    group_blocks = src_ref.at[pl.ds(96 + x * 4, 4)]
    along_x = [
        started(
            remote(
                group_blocks, group_blocks, hub_send.at[4 + k], hub_recv.at[4 + k],
                ((x + k) % NX) * 2 * NZ + z * 2 + core, feat,
            )
        )
        for k in range(1, 4)
    ]
    lax.fori_loop(22, 24, between, 0)
    lax.fori_loop(0, 3, level, 0)
    fill(me // 2)
    halo_copy(sibling).start()

    for copy in loads[4:]:
        copy.wait()
    down = lax.broadcasted_iota(I32, (TILES, TILES), 0)
    along = lax.broadcasted_iota(I32, (TILES, TILES), 1)
    slot_row = lax.broadcasted_iota(I32, (1, TILES), 1)
    key_row = jnp.where(slot_row < live_ref[0], jnp.clip(target_ref[...], 0, BLOCKS - 1), BLOCKS)
    anchor_row = jnp.clip(anchor_ref[...], 0, 111)

    def column(row):
        return jnp.sum(jnp.where(down == along, row, 0), axis=1, keepdims=True)

    key = column(key_row)
    ahead = (key_row < key) | ((key_row == key) & (along < down))
    rank = jnp.sum(jnp.where(ahead, 1, 0), axis=1, keepdims=True)
    placed = rank == along

    def sorted_row(col):
        return jnp.sum(jnp.where(placed, col, 0), axis=0, keepdims=True)

    key_sorted = sorted_row(key)
    slot_col = lax.broadcasted_iota(I32, (TILES, 1), 0)
    table[0:1, 0:TILES] = sorted_row(slot_col)
    table[1:2, 0:TILES] = sorted_row(column(anchor_row))
    table[2:3, 0:TILES] = key_sorted
    blocks_along = lax.broadcasted_iota(I32, (TILES, 128), 1)
    table[3:4, 0:128] = jnp.maximum(
        jnp.sum(jnp.where(key <= blocks_along, 1, 0), axis=0, keepdims=True) - 1, 0
    )
    to_scalars = started(pltpu.make_async_copy(table, order, table_sem))

    def mine(ref):
        part = ref[:, 0:64]
        for k in range(1, NF):
            part = jnp.where(feat == k, ref[:, k * 64 : (k + 1) * 64], part)
        return part

    weights[0] = mine(wself_ref).T
    weights[1] = mine(wneigh_ref).T
    bias[...] = jnp.broadcast_to(mine(bias_ref), (128, 64)).T
    sums[...] = jnp.zeros_like(sums)
    for b in range(32):
        src_ref[b] = feat_ref[:, b * 128 : (b + 1) * 128]
    full_ref[feat] = feat_ref[...]
    to_scalars.wait()
    for copy in along_x:
        copy.wait()

    def arrived(k, _):
        node = (me + k) % NN
        remote(
            outbox.at[node], src_ref.at[32 + node], halo_send.at[node], halo_recv.at[node], node,
            feat,
        ).wait()
        return 0

    lax.fori_loop(1, NN, arrived, 0)

    empty = jnp.zeros((32, 128), BF16)

    def batch(b, total):
        products = []
        for j in range(0, UNROLL, 2):
            slot = b * UNROLL + j
            one = src_ref[order[1, slot]]
            two = src_ref[order[1, slot + 1]]
            rows = jnp.concatenate(
                [jnp.concatenate([one, empty], axis=1), jnp.concatenate([empty, two], axis=1)],
                axis=0,
            )
            pair = jnp.concatenate(
                [values_ref[order[0, slot]], values_ref[order[0, slot + 1]]], axis=1
            )
            product = lax.dot_general(rows, pair, LAST, preferred_element_type=F32)
            products += [product[:32], product[32:]]
        for j in range(UNROLL):
            slot = b * UNROLL + j
            same = order[2, slot] == order[2, jnp.maximum(slot - 1, 0)]
            total = jnp.where(same, total, 0.0) + products[j]
            running[slot] = total
        return total

    lax.fori_loop(0, TILES // UNROLL, batch, jnp.zeros((32, 128), F32))

    width = cot_ref.shape[1] // PARTS

    def at(c):
        return pl.ds(pl.multiple_of(c * width, width), width)

    def direct(c, way):
        slot = (1 - way) // 2
        own = aggs.at[feat, :, at(c)]
        return remote(
            own, own, agg_send.at[slot, c], agg_recv.at[slot, c], me, (feat + way) % NF
        )

    def relay(c):
        way = 1 - 2 * (c % 2)
        theirs = aggs.at[(feat - way) % NF, :, at(c)]
        return remote(
            theirs, theirs, agg_send.at[2, c], agg_recv.at[2, c], me, (feat + way) % NF
        )

    def give(c, _):
        ends = [running[order[3, c * 4 + k]].astype(BF16) for k in range(4)]
        aggs[feat, :, at(c)] = jnp.concatenate(ends, axis=1)
        direct(c, 1).start()
        direct(c, -1).start()
        return 0

    lax.fori_loop(0, PARTS, give, 0)
    for copy in feat_copies:
        copy.wait()

    def own_part(c, _):
        own = full_ref[:, :, at(c)].reshape(128, width)
        own_term[:, at(c)] = (
            jnp.dot(weights[0], own, preferred_element_type=F32) + bias[:, 0:1]
        )
        return 0

    def columns(c):
        span = at(c)
        relay(c).wait()
        own = full_ref[:, :, span].reshape(128, width)
        neigh = aggs[:, :, span].reshape(128, width)
        pre = own_term[:, span] + jnp.dot(weights[1], neigh, preferred_element_type=F32)
        gate = jax.nn.sigmoid(pre)
        hidden_ref[:, span] = (pre * gate).astype(BF16)
        grad = (cot_ref[:, span].astype(F32) * gate * (1.0 + pre * (1.0 - gate))).astype(BF16)
        every = jnp.concatenate([own, neigh, jnp.ones((128, width), BF16)], axis=0)
        sums[...] += lax.dot_general(grad, every, LAST, preferred_element_type=F32)

    def pass_on(c, _):
        direct(c, 1).wait()
        direct(c, -1).wait()
        relay(c).start()
        return 0

    def turn(c, _):
        pass_on(c + 2, 0)
        columns(c)
        return 0

    lax.fori_loop(0, PARTS, own_part, 0)
    lax.fori_loop(0, 2, pass_on, 0)
    lax.fori_loop(0, PARTS - 2, turn, 0)
    columns(PARTS - 2)
    columns(PARTS - 1)

    group = x * 2 + core

    def mate(j):
        return (j // 2) * 2 * NZ + z * 2 + j % 2

    def across(zz):
        return x * 2 * NZ + zz * 2 + core

    for j in range(8):
        pieces[j] = sums[8 * j : 8 * j + 8, :]
    own_piece = pieces.at[group]

    def scatter(k):
        j = (group + k) % 8
        return remote(
            pieces.at[j], inbox.at[group], reduce_send.at[0, j], reduce_recv.at[0, group],
            mate(j), feat,
        )

    def scatter_in(k):
        j = (group + k) % 8
        return remote(
            pieces.at[j], inbox.at[j], reduce_send.at[0, j], reduce_recv.at[0, j], mate(j), feat
        )

    for k in range(1, 8):
        scatter(k).start()
    inbox[group] = own_piece[...]
    for k in range(1, 8):
        scatter_in(k).wait()
    crossed = inbox[0]
    for j in range(1, 8):
        crossed = crossed + inbox[j]
    partial[...] = crossed
    crossbox[z] = crossed

    def cross(k):
        zz = (z + k) % NZ
        return remote(
            partial, crossbox.at[z], reduce_send.at[1, zz], reduce_recv.at[1, z], across(zz), feat
        )

    def cross_in(k):
        zz = (z + k) % NZ
        return remote(
            partial, crossbox.at[zz], reduce_send.at[1, zz], reduce_recv.at[1, zz], across(zz),
            feat,
        )

    for k in range(1, 8):
        cross(k).start()
    for k in range(1, 8):
        cross_in(k).wait()
    total = crossbox[0]
    for j in range(1, 8):
        total = total + crossbox[j]
    totals[group] = total

    def spread(k):
        j = (group + k) % 8
        return remote(
            totals.at[group], totals.at[group], reduce_send.at[2, j], reduce_recv.at[2, group],
            mate(j), feat,
        )

    def spread_in(k):
        j = (group + k) % 8
        return remote(
            totals.at[group], totals.at[j], reduce_send.at[2, j], reduce_recv.at[2, j], mate(j),
            feat,
        )

    for k in range(1, 8):
        spread(k).start()
    for k in range(1, 8):
        spread_in(k).wait()
    done = totals[...].reshape(64, 384)
    gself_ref[...] = done[:, 0:128]
    gneigh_ref[...] = done[:, 128:256]
    gbias_ref[...] = done[:, 256:384].T[0:1, :]


def local(
    features, w_self, w_neigh, hidden_bias, cotangent, hub_local, send_rows, send_count,
    tile_values, tile_target, tile_anchor, tile_count,
):
    cols = features.shape[1]
    operands = (
        features, w_self, w_neigh, hidden_bias.reshape(1, -1), cotangent, hub_local, send_rows[0],
        send_count, tile_values, tile_target, tile_anchor, tile_count,
    )
    vmem = pl.BlockSpec(memory_space=pltpu.VMEM)
    scalars = (7, 11)
    hidden, grad_self, grad_neigh, bias_grad = pl.pallas_call(
        layer_kernel,
        name="layer",
        out_shape=(
            jax.ShapeDtypeStruct((64, cols), BF16),
            jax.ShapeDtypeStruct((64, 128), F32),
            jax.ShapeDtypeStruct((64, 128), F32),
            jax.ShapeDtypeStruct((1, 64), F32),
        ),
        in_specs=[pl.BlockSpec(memory_space=pl.ANY)] * 12,
        out_specs=(vmem,) * 4,
        scratch_shapes=[
            (pltpu.SMEM if i in scalars else pltpu.VMEM)(operand.shape, operand.dtype)
            for i, operand in enumerate(operands)
        ]
        + [
            pltpu.VMEM((112, 32, 128), BF16),
            pltpu.VMEM((NF, 32, cols), BF16),
            pltpu.VMEM((512, 256), BF16),
            pltpu.VMEM((NN, 32, 128), BF16),
            pltpu.VMEM((32, 128), BF16),
            pltpu.VMEM((32, 128), BF16),
            pltpu.VMEM((32, 128), BF16),
            pltpu.VMEM((32, 128), BF16),
            pltpu.VMEM((8, 384), I32),
            pltpu.SMEM((8, 384), I32),
            pltpu.VMEM((TILES, 32, 128), F32),
            pltpu.VMEM((NF, 32, cols), BF16),
            pltpu.VMEM((2, 64, 128), BF16),
            pltpu.VMEM((64, 128), F32),
            pltpu.VMEM((64, cols), F32),
            pltpu.VMEM((64, 384), F32),
            pltpu.VMEM((8, 8, 384), F32),
            pltpu.VMEM((8, 8, 384), F32),
            pltpu.VMEM((8, 384), F32),
            pltpu.VMEM((8, 8, 384), F32),
            pltpu.VMEM((8, 8, 384), F32),
            pltpu.SemaphoreType.DMA((12,)),
            pltpu.SemaphoreType.DMA,
            pltpu.SemaphoreType.DMA((NN,)),
            pltpu.SemaphoreType.DMA((NN,)),
            pltpu.SemaphoreType.DMA((NF,)),
            pltpu.SemaphoreType.DMA((NF,)),
            pltpu.SemaphoreType.DMA((8,)),
            pltpu.SemaphoreType.DMA((8,)),
            pltpu.SemaphoreType.DMA((3, PARTS)),
            pltpu.SemaphoreType.DMA((3, PARTS)),
            pltpu.SemaphoreType.DMA((3, 8)),
            pltpu.SemaphoreType.DMA((3, 8)),
        ],
        compiler_params=pltpu.CompilerParams(
            collective_id=0, has_side_effects=True, vmem_limit_bytes=56 * 2**20
        ),
    )(*operands)
    return hidden, grad_self.T, grad_neigh.T, bias_grad.reshape(-1)


def solution(mesh):
    in_specs = (
        P("feat", "nodes"), P(), P(), P(), P("feat", "nodes"), P("nodes", None),
        P("nodes", None, None), P("nodes", None), P("nodes", None, None), P("nodes", None),
        P("nodes", None), P("nodes"),
    )
    out_specs = (P("feat", "nodes"), P(None, "feat"), P(None, "feat"), P("feat"))
    return jax.shard_map(local, mesh=mesh, in_specs=in_specs, out_specs=out_specs, check_vma=False)
```

time: 417 us -> 77.7 us (0.19)
  waiting for transfers between devices: 174 us -> 0 us
  blocking collectives: 134 us -> 0 us
  Pallas kernels: 0 us -> 70.3 us
  local copies, waits for them, and re-layouts: 39.6 us -> 5.79 us
  starting transfers between devices: 23.4 us -> 0 us
  matrix products: 21.7 us -> 0 us
  between operations: 14.7 us -> 1.29 us
  other arithmetic: 9.63 us -> 0 us
    psum x1 -> x0, blocking collectives: 127 us -> none  [local(): weight_total, bias_grad = lax.psum((weight_part, bias_part), 'nodes')]
    reduce_scatter x1 -> x0, waiting for transfers between devices: 79.5 us -> none  [local(): lax.psum_scatter(own_term + lax.dot_general(neigh_rows, aggregate, contra...]
    pallas_call x0 -> x1, Pallas kernels: none -> 70.3 us  [local(): pl.pallas_call(layer_kernel, name='layer', out_shape=(jax.ShapeDtypeStruc...]
    psum x1 -> x0, waiting for transfers between devices: 48 us -> none  [local(): weight_total, bias_grad = lax.psum((weight_part, bias_part), 'nodes')]
    all_gather x1 -> x0, waiting for transfers between devices: 33.2 us -> none  [local(): grad_piece = lax.all_gather(pre_grad, 'feat', axis=0, tiled=True)]
    gather x7 -> x0, local copies, waits for them, and re-layouts: 27.9 us -> none  [the longest x2 24.9 us: local(): jnp.take(features, send_rows[0].reshape(-1), axis=1)]
    all_to_all x2 -> x0, starting transfers between devices: 23.3 us -> none  [the longest x1 13 us: local(): lax.all_to_all(copies, 'nodes', split_axis=1, concat_axis=1, tiled=True)]
    dot_general x12 -> x0, matrix products: 21.7 us -> none  [the longest x4 7.66 us: one_turn(): jnp.einsum('ftk,tik->fti', picked, tile_block, preferred_element_type=jnp...]
  transfers between devices with their start and end apart: 5 -> 0, of which waited for: 4 -> 0; matrix products, arithmetic and copies ran while one was open for 7% -> 0% of each run, Pallas kernels for 0% -> 0%
where the time goes in v2:
time: 77.7 us; the launch traced here: 77.4 us
  Pallas kernels  70.3 us (90%)
  local copies, waits for them, and re-layouts  5.79 us (7%)
  between operations  1.29 us (2%)
    pallas_call x1, Pallas kernels, local(): pl.pallas_call(layer_kernel, name='layer', out_shape=(jax.ShapeDtypeStruc...  70.3 us
    unnamed x4, local copies, waits for them, and re-layouts  5.79 us

profile of v2, /device:TPU:1, one launch (start us, length us, event | category | flops | bytes accessed | tf_op | source)
XLA Modules:
  0.0 77.4 jit_solution(13814899174837436024)
XLA Ops:
  1.3 70.3 %layer.1 = (bf16[64,4096]{1,0:T(8,128)(2,1)}, f32[64,128]{1,0:T(8,128)}, f32[64,128]{1,0:T(8,128)}, f32[1,64]{1,0:T(1,128)}) custom-call(bf16[32,4096]{1,0:T(8,128)(2,1)} %feat_in.1, bf16[128,256]{1,0:T(8,128)(2,1)} %wself_in.1, bf16[128,256]{1,0:T(8,128)(2,1)} %wneigh_in.1, f32[1,256]{1,0:T(1,128)} %bitcast.8, bf16[64,4096]{1,0:T(8,128)(2,1)} %cot_in.1, ...), custom_call_target="tpu_custom_call" | custom-call | tf_op jit(solution)/shard_map/layer/pallas_call | solution.py:431
  71.6 1.9 %copy.21 = bf16[64,4096]{1,0:T(8,128)(2,1)} copy(bf16[64,4096]{1,0:T(8,128)(2,1)} %get-tuple-element.16) | data formatting | bytes 1048576
  73.5 1.4 %copy.22 = f32[128,64]{0,1:T(8,128)} copy(f32[128,64]{0,1:T(8,128)} %bitcast.7) | data formatting | bytes 65536
  74.9 1.4 %copy.23 = f32[128,64]{0,1:T(8,128)} copy(f32[128,64]{0,1:T(8,128)} %bitcast.6) | data formatting | bytes 65536
  76.2 1.2 %copy.24 = f32[64]{0:T(128)} copy(f32[64]{0:T(128)} %bitcast.9) | data formatting | bytes 512

commit v3 on v2

--- a/solution.py
+++ b/solution.py
@@ -10,6 +10,8 @@
 TILES = 352
 BLOCKS = 32
 UNROLL = 32
+FLIPS = 16
+FAR_FIRST = (4, 3, 5, 2, 6, 1, 7)
 PARTS = 8
 LAST = (((1,), (1,)), ((), ()))
 F32 = jnp.float32
@@ -40,7 +42,7 @@
     anchor_in, live_in, hidden_ref, gself_ref, gneigh_ref, gbias_ref,
     feat_ref, wself_ref, wneigh_ref, bias_ref, cot_ref, hub_ref, rows_ref, count_ref, values_ref,
     target_ref, anchor_ref, live_ref,
-    src_ref, full_ref, stacked, outbox, hub0, hub0_in, hub1, hub1_in, table, order, running,
+    src_ref, full_ref, stacked, outbox, hub0, hub0_in, hub_parts, table, order, running,
     aggs, weights, bias, own_term, sums, pieces, inbox, partial, crossbox, totals,
     load_sem, table_sem, halo_send, halo_recv, feat_send, feat_recv, hub_send, hub_recv,
     agg_send, agg_recv, reduce_send, reduce_recv,
@@ -77,24 +79,30 @@
         stacked[h * 32 : (h + 1) * 32, :] = feat_ref[:, h * 256 : (h + 1) * 256]
     lane = lax.broadcasted_iota(I32, (1, 128), 1)
 
-    def pick(index):
-        low = index & 255
-        high = index >> 8
-        hot = (lax.broadcasted_iota(I32, (256, 256), 0) == low).astype(F32).astype(BF16)
-        parts = jnp.dot(stacked[...], hot, preferred_element_type=F32)
-        out = jnp.zeros((32, 256), F32)
-        for h in range(16):
-            out = jnp.where(high == h, parts[h * 32 : (h + 1) * 32], out)
-        return out.astype(BF16)
-
-    def fill(chip):
-        first = jnp.where(lane < count_ref[0, 2 * chip], rows_ref[pl.ds(2 * chip, 1), :], -1)
-        second = jnp.where(
-            lane < count_ref[0, 2 * chip + 1], rows_ref[pl.ds(2 * chip + 1, 1), :], -1
-        )
-        rows = pick(jnp.concatenate([first, second], axis=1))
-        outbox[2 * chip] = rows[:, :128]
-        outbox[2 * chip + 1] = rows[:, 128:]
+    def pick(indices):
+        down256 = lax.broadcasted_iota(I32, (256, 256), 0)
+        hots = [(down256 == (index & 255)).astype(F32).astype(BF16) for index in indices]
+        parts = [jnp.dot(stacked[...], hot, preferred_element_type=F32) for hot in hots]
+        picked = []
+        for index, part in zip(indices, parts):
+            high = index >> 8
+            out = jnp.zeros((32, 256), F32)
+            for h in range(16):
+                out = jnp.where(high == h, part[h * 32 : (h + 1) * 32], out)
+            picked.append(out.astype(BF16))
+        return picked
+
+    def fill(chips):
+        indices = []
+        for chip in chips:
+            pair = [
+                jnp.where(lane < count_ref[0, node], rows_ref[pl.ds(node, 1), :], -1)
+                for node in (2 * chip, 2 * chip + 1)
+            ]
+            indices.append(jnp.concatenate(pair, axis=1))
+        for chip, rows in zip(chips, pick(indices)):
+            outbox[2 * chip] = rows[:, :128]
+            outbox[2 * chip + 1] = rows[:, 128:]
 
     def halo_copy(node):
         return remote(
@@ -109,34 +117,23 @@
         halo_copy(2 * chip).start()
         halo_copy(2 * chip + 1).start()
 
-    def opposite(k, _):
-        fill(chip_at(k, 4))
-        return 0
-
-    def opposite_send(k, _):
-        send(chip_at(k, 4))
-        return 0
-
-    def between(j, _):
-        turn = j % 8
-        dz = 4 + (2 * (turn % 2) - 1) * (1 + j // 8)
-        chip = chip_at(turn // 2, dz)
-        fill(chip)
-        send(chip)
-        return 0
-
-    def level(k, _):
-        chip = chip_at(k, 0)
-        fill(chip)
-        send(chip)
+    def between(i, _):
+        chips = [
+            chip_at(2 * (i % 2) + j // 2, 4 + (2 * (j % 2) - 1) * (1 + i // 2)) for j in range(4)
+        ]
+        fill(chips)
+        for chip in chips:
+            send(chip)
         return 0
 
     sibling = me + 1 - 2 * core
     hubs = jnp.concatenate([hub_ref[...]] * 4, axis=1)
-    hubs = jnp.where(lane // 32 == me % 4, hubs, -1)
-    hub0[...] = pick(jnp.concatenate([hubs, jnp.full_like(hubs, -1)], axis=1))[:, :128]
+    hubs = jnp.where(lane // 32 % 2 == core, hubs, -1)
+    own_hubs = pick([jnp.concatenate([hubs, jnp.full_like(hubs, -1)], axis=1)])[0][:, :128]
+    hub0[...] = jnp.where(lane < 64, own_hubs[:16], own_hubs[16:])
     src_ref[32 + me] = jnp.zeros((32, 128), BF16)
-    lax.fori_loop(0, 4, opposite, 0)
+    opposite = [chip_at(k, 4) for k in range(4)]
+    fill(opposite)
     pl.semaphore_wait(barrier, NN - 1 + NF - 1)
 
     first = started(remote(hub0, hub0_in, hub_send.at[0], hub_recv.at[0], sibling, feat))
@@ -149,44 +146,28 @@
         )
         for k in range(1, NF)
     ]
-    lax.fori_loop(0, 4, opposite_send, 0)
-    lax.fori_loop(0, 2, between, 0)
+    for chip in opposite:
+        send(chip)
+    lax.fori_loop(0, 1, between, 0)
     first.wait()
-    hub1[...] = hub0[...] + hub0_in[...]
-    across_pair = x * 2 * NZ + (z + 1 - 2 * (z % 2)) * 2 + core
-    second = started(remote(hub1, hub1_in, hub_send.at[1], hub_recv.at[1], across_pair, feat))
-    lax.fori_loop(2, 9, between, 0)
-    second.wait()
-    block = 96 + me // 4
-    src_ref[block] = hub1[...] + hub1_in[...]
-    along_z = [
-        started(
-            remote(
-                src_ref.at[block], src_ref.at[block], hub_send.at[1 + k], hub_recv.at[1 + k],
-                x * 2 * NZ + ((z + 2 * k) % NZ) * 2 + core, feat,
-            )
-        )
-        for k in range(1, 4)
-    ]
-    lax.fori_loop(9, 22, between, 0)
-    for copy in along_z:
-        copy.wait()
-    group_blocks = src_ref.at[pl.ds(96 + x * 4, 4)]
-    along_x = [
-        started(
-            remote(
-                group_blocks, group_blocks, hub_send.at[4 + k], hub_recv.at[4 + k],
-                ((x + k) % NX) * 2 * NZ + z * 2 + core, feat,
-            )
-        )
-        for k in range(1, 4)
-    ]
-    lax.fori_loop(22, 24, between, 0)
-    lax.fori_loop(0, 3, level, 0)
-    fill(me // 2)
+    hub_parts[x, z] = hub0[...] + hub0_in[...]
+
+    def chip_hubs(k, zz):
+        return remote(
+            hub_parts.at[x, z], hub_parts.at[x, zz], hub_send.at[k], hub_recv.at[k],
+            x * 2 * NZ + ((z + k) % NZ) * 2 + core, feat,
+        )
+
+    for k in FAR_FIRST:
+        chip_hubs(k, z).start()
+    lax.fori_loop(1, 6, between, 0)
+    level = [chip_at(k, 0) for k in range(3)] + [me // 2]
+    fill(level)
+    for chip in level[:3]:
+        send(chip)
     halo_copy(sibling).start()
 
-    for copy in loads[4:]:
+    for copy in loads[4:-1]:
         copy.wait()
     down = lax.broadcasted_iota(I32, (TILES, TILES), 0)
     along = lax.broadcasted_iota(I32, (TILES, TILES), 1)
@@ -216,6 +197,18 @@
     )
     to_scalars = started(pltpu.make_async_copy(table, order, table_sem))
 
+    for k in range(1, NZ):
+        chip_hubs(k, (z - k) % NZ).wait()
+
+    def row_hubs(k, xx):
+        return remote(
+            hub_parts.at[x], hub_parts.at[xx], hub_send.at[7 + k], hub_recv.at[7 + k],
+            ((x + k) % NX) * 2 * NZ + z * 2 + core, feat,
+        )
+
+    for k in (2, 1, 3):
+        row_hubs(k, x).start()
+
     def mine(ref):
         part = ref[:, 0:64]
         for k in range(1, NF):
@@ -230,8 +223,22 @@
         src_ref[b] = feat_ref[:, b * 128 : (b + 1) * 128]
     full_ref[feat] = feat_ref[...]
     to_scalars.wait()
-    for copy in along_x:
-        copy.wait()
+    loads[-1].wait()
+
+    def flip(b, _):
+        tiles = [values_ref[b * FLIPS + j].T for j in range(FLIPS)]
+        for j in range(FLIPS):
+            values_ref[b * FLIPS + j] = tiles[j]
+        return 0
+
+    lax.fori_loop(0, TILES // FLIPS, flip, 0)
+    for k in range(1, NX):
+        row_hubs(k, (x - k) % NX).wait()
+    for b in range(16):
+        even = hub_parts[b // 4, 2 * (b % 4)]
+        odd = hub_parts[b // 4, 2 * (b % 4) + 1]
+        src_ref[96 + b, 0:16, :] = jnp.concatenate([even[:, :64], odd[:, :64]], axis=1)
+        src_ref[96 + b, 16:32, :] = jnp.concatenate([even[:, 64:], odd[:, 64:]], axis=1)
 
     def arrived(k, _):
         node = (me + k) % NN
@@ -256,9 +263,9 @@
                 axis=0,
             )
             pair = jnp.concatenate(
-                [values_ref[order[0, slot]], values_ref[order[0, slot + 1]]], axis=1
+                [values_ref[order[0, slot]], values_ref[order[0, slot + 1]]], axis=0
             )
-            product = lax.dot_general(rows, pair, LAST, preferred_element_type=F32)
+            product = jnp.dot(rows, pair, preferred_element_type=F32)
             products += [product[:32], product[32:]]
         for j in range(UNROLL):
             slot = b * UNROLL + j
@@ -276,21 +283,21 @@
 
     def direct(c, way):
         slot = (1 - way) // 2
-        own = aggs.at[feat, :, at(c)]
+        own = aggs.at[c, feat]
         return remote(
             own, own, agg_send.at[slot, c], agg_recv.at[slot, c], me, (feat + way) % NF
         )
 
     def relay(c):
         way = 1 - 2 * (c % 2)
-        theirs = aggs.at[(feat - way) % NF, :, at(c)]
+        theirs = aggs.at[c, (feat - way) % NF]
         return remote(
             theirs, theirs, agg_send.at[2, c], agg_recv.at[2, c], me, (feat + way) % NF
         )
 
     def give(c, _):
         ends = [running[order[3, c * 4 + k]].astype(BF16) for k in range(4)]
-        aggs[feat, :, at(c)] = jnp.concatenate(ends, axis=1)
+        aggs[c, feat] = jnp.concatenate(ends, axis=1)
         direct(c, 1).start()
         direct(c, -1).start()
         return 0
@@ -310,7 +317,7 @@
         span = at(c)
         relay(c).wait()
         own = full_ref[:, :, span].reshape(128, width)
-        neigh = aggs[:, :, span].reshape(128, width)
+        neigh = aggs[c].reshape(128, width)
         pre = own_term[:, span] + jnp.dot(weights[1], neigh, preferred_element_type=F32)
         gate = jax.nn.sigmoid(pre)
         hidden_ref[:, span] = (pre * gate).astype(BF16)
@@ -325,15 +332,12 @@
         return 0
 
     def turn(c, _):
-        pass_on(c + 2, 0)
         columns(c)
         return 0
 
     lax.fori_loop(0, PARTS, own_part, 0)
-    lax.fori_loop(0, 2, pass_on, 0)
-    lax.fori_loop(0, PARTS - 2, turn, 0)
-    columns(PARTS - 2)
-    columns(PARTS - 1)
+    lax.fori_loop(0, PARTS, pass_on, 0)
+    lax.fori_loop(0, PARTS, turn, 0)
 
     group = x * 2 + core
 
@@ -360,7 +364,7 @@
             pieces.at[j], inbox.at[j], reduce_send.at[0, j], reduce_recv.at[0, j], mate(j), feat
         )
 
-    for k in range(1, 8):
+    for k in FAR_FIRST:
         scatter(k).start()
     inbox[group] = own_piece[...]
     for k in range(1, 8):
@@ -384,7 +388,7 @@
             feat,
         )
 
-    for k in range(1, 8):
+    for k in FAR_FIRST:
         cross(k).start()
     for k in range(1, 8):
         cross_in(k).wait()
@@ -407,7 +411,7 @@
             feat,
         )
 
-    for k in range(1, 8):
+    for k in FAR_FIRST:
         spread(k).start()
     for k in range(1, 8):
         spread_in(k).wait()
@@ -424,8 +428,11 @@
     cols = features.shape[1]
     operands = (
         features, w_self, w_neigh, hidden_bias.reshape(1, -1), cotangent, hub_local, send_rows[0],
-        send_count, tile_values, tile_target, tile_anchor, tile_count,
+        send_count, tile_values, tile_target, tile_anchor,
     )
+    operands = tuple(
+        pltpu.with_memory_space_constraint(operand, pltpu.MemorySpace.HBM) for operand in operands
+    ) + (tile_count,)
     vmem = pl.BlockSpec(memory_space=pltpu.VMEM)
     scalars = (7, 11)
     hidden, grad_self, grad_neigh, bias_grad = pl.pallas_call(
@@ -448,14 +455,13 @@
             pltpu.VMEM((NF, 32, cols), BF16),
             pltpu.VMEM((512, 256), BF16),
             pltpu.VMEM((NN, 32, 128), BF16),
-            pltpu.VMEM((32, 128), BF16),
-            pltpu.VMEM((32, 128), BF16),
-            pltpu.VMEM((32, 128), BF16),
-            pltpu.VMEM((32, 128), BF16),
+            pltpu.VMEM((16, 128), BF16),
+            pltpu.VMEM((16, 128), BF16),
+            pltpu.VMEM((NX, NZ, 16, 128), BF16),
             pltpu.VMEM((8, 384), I32),
             pltpu.SMEM((8, 384), I32),
             pltpu.VMEM((TILES, 32, 128), F32),
-            pltpu.VMEM((NF, 32, cols), BF16),
+            pltpu.VMEM((PARTS, NF, 32, cols // PARTS), BF16),
             pltpu.VMEM((2, 64, 128), BF16),
             pltpu.VMEM((64, 128), F32),
             pltpu.VMEM((64, cols), F32),
@@ -471,15 +477,15 @@
             pltpu.SemaphoreType.DMA((NN,)),
             pltpu.SemaphoreType.DMA((NF,)),
             pltpu.SemaphoreType.DMA((NF,)),
-            pltpu.SemaphoreType.DMA((8,)),
-            pltpu.SemaphoreType.DMA((8,)),
+            pltpu.SemaphoreType.DMA((11,)),
+            pltpu.SemaphoreType.DMA((11,)),
             pltpu.SemaphoreType.DMA((3, PARTS)),
             pltpu.SemaphoreType.DMA((3, PARTS)),
             pltpu.SemaphoreType.DMA((3, 8)),
             pltpu.SemaphoreType.DMA((3, 8)),
         ],
         compiler_params=pltpu.CompilerParams(
-            collective_id=0, has_side_effects=True, vmem_limit_bytes=56 * 2**20
+            collective_id=0, has_side_effects=True, vmem_limit_bytes=40 * 2**20
         ),
     )(*operands)
     return hidden, grad_self.T, grad_neigh.T, bias_grad.reshape(-1)

time: 77.7 us -> 62.9 us (0.81)
  Pallas kernels: 70.3 us -> 59 us
  local copies, waits for them, and re-layouts: 5.79 us -> 2.54 us
    pallas_call x1, Pallas kernels: 70.3 us -> 59 us  [local(): pl.pallas_call(layer_kernel, name='layer', out_shape=(jax.ShapeDtypeStruc...]
    unnamed x4, local copies, waits for them, and re-layouts: 5.79 us -> 2.54 us
where the time goes in v3:
time: 62.9 us; the launch traced here: 62.8 us
  Pallas kernels  59 us (94%)
  local copies, waits for them, and re-layouts  2.54 us (4%)
  between operations  1.29 us (2%)
    pallas_call x1, Pallas kernels, local(): pl.pallas_call(layer_kernel, name='layer', out_shape=(jax.ShapeDtypeStruc...  59 us
    unnamed x4, local copies, waits for them, and re-layouts  2.54 us

profile of v3, /device:TPU:1, one launch (start us, length us, event | category | flops | bytes accessed | tf_op | source)
XLA Modules:
  0.0 62.8 jit_solution(8346107520167557661)
XLA Ops:
  1.3 59.0 %layer.1 = (bf16[64,4096]{1,0:T(8,128)(2,1)S(1)}, f32[64,128]{1,0:T(8,128)S(1)}, f32[64,128]{1,0:T(8,128)S(1)}, f32[1,64]{1,0:T(1,128)S(1)}) custom-call(bf16[32,4096]{1,0:T(8,128)(2,1)} %feat_in.1, bf16[128,256]{1,0:T(8,128)(2,1)} %wself_in.1, bf16[128,256]{1,0:T(8,128)(2,1)} %wneigh_in.1, f32[1,256]{1,0:T(1,128)} %bitcast.9, bf16[64,4096]{1,0:T(8,128)(2,1)} %cot_in.1, ...), custom_call_target="tpu_custom_call" | custom-call | tf_op jit(solution)/shard_map/layer/pallas_call | solution.py:438
  60.3 0.8 %copy.21 = bf16[64,4096]{1,0:T(8,128)(2,1)} copy(bf16[64,4096]{1,0:T(8,128)(2,1)S(1)} %get-tuple-element.16) | data formatting | bytes 1048576
  61.1 0.6 copy.22
  61.7 0.6 copy.23
  62.3 0.5 copy.24

commit v4 on v3

--- a/solution.py
+++ b/solution.py
@@ -13,6 +13,7 @@
 FLIPS = 16
 FAR_FIRST = (4, 3, 5, 2, 6, 1, 7)
 PARTS = 8
+RELAYED = 6
 LAST = (((1,), (1,)), ((), ()))
 F32 = jnp.float32
 BF16 = jnp.bfloat16
@@ -39,7 +40,7 @@
 
 def layer_kernel(
     feat_in, wself_in, wneigh_in, bias_in, cot_in, hub_in, rows_in, count_in, values_in, target_in,
-    anchor_in, live_in, hidden_ref, gself_ref, gneigh_ref, gbias_ref,
+    anchor_in, live_in, hidden_ref, grads_ref,
     feat_ref, wself_ref, wneigh_ref, bias_ref, cot_ref, hub_ref, rows_ref, count_ref, values_ref,
     target_ref, anchor_ref, live_ref,
     src_ref, full_ref, stacked, outbox, hub0, hub0_in, hub_parts, table, order, running,
@@ -117,10 +118,13 @@
         halo_copy(2 * chip).start()
         halo_copy(2 * chip + 1).start()
 
-    def between(i, _):
-        chips = [
+    def between_chips(i):
+        return [
             chip_at(2 * (i % 2) + j // 2, 4 + (2 * (j % 2) - 1) * (1 + i // 2)) for j in range(4)
         ]
+
+    def between(i, _):
+        chips = between_chips(i)
         fill(chips)
         for chip in chips:
             send(chip)
@@ -240,15 +244,26 @@
         src_ref[96 + b, 0:16, :] = jnp.concatenate([even[:, :64], odd[:, :64]], axis=1)
         src_ref[96 + b, 16:32, :] = jnp.concatenate([even[:, 64:], odd[:, 64:]], axis=1)
 
-    def arrived(k, _):
-        node = (me + k) % NN
+    def arrived(node):
         remote(
             outbox.at[node], src_ref.at[32 + node], halo_send.at[node], halo_recv.at[node], node,
             feat,
-        ).wait()
-        return 0
-
-    lax.fori_loop(1, NN, arrived, 0)
+        ).wait_recv()
+
+    def between_arrived(i, _):
+        for chip in between_chips(i):
+            arrived(2 * chip)
+            arrived(2 * chip + 1)
+        return 0
+
+    for chip in opposite:
+        arrived(2 * chip)
+        arrived(2 * chip + 1)
+    lax.fori_loop(0, 6, between_arrived, 0)
+    for chip in level[:3]:
+        arrived(2 * chip)
+        arrived(2 * chip + 1)
+    arrived(sibling)
 
     empty = jnp.zeros((32, 128), BF16)
 
@@ -295,14 +310,37 @@
             theirs, theirs, agg_send.at[2, c], agg_recv.at[2, c], me, (feat + way) % NF
         )
 
+    def over(c):
+        own = aggs.at[c, feat]
+        return remote(own, own, agg_send.at[2, c], agg_recv.at[2, c], me, (feat + 2) % NF)
+
     def give(c, _):
         ends = [running[order[3, c * 4 + k]].astype(BF16) for k in range(4)]
         aggs[c, feat] = jnp.concatenate(ends, axis=1)
+
+        return 0
+
+    def give_all(c, _):
+        give(c, 0)
+        over(c).start()
         direct(c, 1).start()
         direct(c, -1).start()
         return 0
 
-    lax.fori_loop(0, PARTS, give, 0)
+    def give_near(c, _):
+        give(c, 0)
+        direct(c, 1).start()
+        direct(c, -1).start()
+        return 0
+
+    lax.fori_loop(RELAYED, PARTS, give_all, 0)
+    lax.fori_loop(0, RELAYED, give_near, 0)
+
+    def halo_left(k, _):
+        halo_copy((me + k) % NN).wait_send()
+        return 0
+
+    lax.fori_loop(1, NN, halo_left, 0)
     for copy in feat_copies:
         copy.wait()
 
@@ -315,7 +353,7 @@
 
     def columns(c):
         span = at(c)
-        relay(c).wait()
+        relay(c).wait_recv()
         own = full_ref[:, :, span].reshape(128, width)
         neigh = aggs[c].reshape(128, width)
         pre = own_term[:, span] + jnp.dot(weights[1], neigh, preferred_element_type=F32)
@@ -326,18 +364,28 @@
         sums[...] += lax.dot_general(grad, every, LAST, preferred_element_type=F32)
 
     def pass_on(c, _):
-        direct(c, 1).wait()
-        direct(c, -1).wait()
+        direct(c, 1).wait_recv()
+        direct(c, -1).wait_recv()
         relay(c).start()
         return 0
 
-    def turn(c, _):
+    def final(c, _):
         columns(c)
         return 0
 
+    def drain(c, _):
+        direct(c, 1).wait_send()
+        direct(c, -1).wait_send()
+        relay(c).wait_send()
+        return 0
+
     lax.fori_loop(0, PARTS, own_part, 0)
-    lax.fori_loop(0, PARTS, pass_on, 0)
-    lax.fori_loop(0, PARTS, turn, 0)
+    lax.fori_loop(0, RELAYED, pass_on, 0)
+    for c in range(RELAYED, PARTS):
+        direct(c, 1).wait_recv()
+        direct(c, -1).wait_recv()
+    lax.fori_loop(RELAYED, PARTS, final, 0)
+    lax.fori_loop(0, RELAYED, final, 0)
 
     group = x * 2 + core
 
@@ -367,6 +415,7 @@
     for k in FAR_FIRST:
         scatter(k).start()
     inbox[group] = own_piece[...]
+    lax.fori_loop(0, PARTS, drain, 0)
     for k in range(1, 8):
         scatter_in(k).wait()
     crossed = inbox[0]
@@ -415,10 +464,23 @@
         spread(k).start()
     for k in range(1, 8):
         spread_in(k).wait()
-    done = totals[...].reshape(64, 384)
-    gself_ref[...] = done[:, 0:128]
-    gneigh_ref[...] = done[:, 128:256]
-    gbias_ref[...] = done[:, 256:384].T[0:1, :]
+    grads_ref[...] = totals[...].reshape(64, 384)
+
+
+def finish_kernel(hidden_ref, grads_ref, hidden_out, gself_out, gneigh_out, gbias_out, bias, sem):
+    copies = [
+        started(pltpu.make_async_copy(src, dst, sem.at[i]))
+        for i, (src, dst) in enumerate(
+            (
+                (hidden_ref, hidden_out), (grads_ref.at[:, 0:128], gself_out),
+                (grads_ref.at[:, 128:256], gneigh_out),
+            )
+        )
+    ]
+    bias[...] = grads_ref[:, 256:384].T[0:1, :]
+    copies.append(started(pltpu.make_async_copy(bias, gbias_out, sem.at[3])))
+    for copy in copies:
+        copy.wait()
 
 
 def local(
@@ -435,17 +497,15 @@
     ) + (tile_count,)
     vmem = pl.BlockSpec(memory_space=pltpu.VMEM)
     scalars = (7, 11)
-    hidden, grad_self, grad_neigh, bias_grad = pl.pallas_call(
+    hidden, grads = pl.pallas_call(
         layer_kernel,
         name="layer",
         out_shape=(
             jax.ShapeDtypeStruct((64, cols), BF16),
-            jax.ShapeDtypeStruct((64, 128), F32),
-            jax.ShapeDtypeStruct((64, 128), F32),
-            jax.ShapeDtypeStruct((1, 64), F32),
+            jax.ShapeDtypeStruct((64, 384), F32),
         ),
         in_specs=[pl.BlockSpec(memory_space=pl.ANY)] * 12,
-        out_specs=(vmem,) * 4,
+        out_specs=(vmem,) * 2,
         scratch_shapes=[
             (pltpu.SMEM if i in scalars else pltpu.VMEM)(operand.shape, operand.dtype)
             for i, operand in enumerate(operands)
@@ -488,6 +548,20 @@
             collective_id=0, has_side_effects=True, vmem_limit_bytes=40 * 2**20
         ),
     )(*operands)
+    hidden, grad_self, grad_neigh, bias_grad = pl.pallas_call(
+        finish_kernel,
+        name="finish",
+        out_shape=(
+            jax.ShapeDtypeStruct((64, cols), BF16),
+            jax.ShapeDtypeStruct((64, 128), F32),
+            jax.ShapeDtypeStruct((64, 128), F32),
+            jax.ShapeDtypeStruct((1, 64), F32),
+        ),
+        in_specs=[vmem] * 2,
+        out_specs=(pl.BlockSpec(memory_space=pl.ANY),) * 4,
+        scratch_shapes=[pltpu.VMEM((1, 64), F32), pltpu.SemaphoreType.DMA((4,))],
+        compiler_params=pltpu.CompilerParams(vmem_limit_bytes=4 * 2**20),
+    )(hidden, grads)
     return hidden, grad_self.T, grad_neigh.T, bias_grad.reshape(-1)
 
 

time: 62.9 us -> 61 us (0.970)
  local copies, waits for them, and re-layouts: 2.54 us -> 0 us
    unnamed x4 -> x0, local copies, waits for them, and re-layouts: 2.54 us -> none
    pallas_call x0 -> x1, Pallas kernels: none -> 0.84 us  [local(): pl.pallas_call(finish_kernel, name='finish', out_shape=(jax.ShapeDtypeStr...]
where the time goes in v4:
time: 61 us; the launch traced here: 60.9 us
  Pallas kernels  59.6 us (98%)
  between operations  1.29 us (2%)
    pallas_call x1, Pallas kernels, local(): pl.pallas_call(layer_kernel, name='layer', out_shape=(jax.ShapeDtypeStruc...  58.8 us

profile of v4, /device:TPU:1, one launch (start us, length us, event | category | flops | bytes accessed | tf_op | source)
XLA Modules:
  0.0 60.9 jit_solution(8939485753919444137)
XLA Ops:
  1.3 58.8 %layer.1 = (bf16[64,4096]{1,0:T(8,128)(2,1)S(1)}, f32[64,384]{1,0:T(8,128)S(1)}) custom-call(bf16[32,4096]{1,0:T(8,128)(2,1)} %feat_in.1, bf16[128,256]{1,0:T(8,128)(2,1)} %wself_in.1, bf16[128,256]{1,0:T(8,128)(2,1)} %wneigh_in.1, f32[1,256]{1,0:T(1,128)} %bitcast.6, bf16[64,4096]{1,0:T(8,128)(2,1)} %cot_in.1, s32[1,32]{1,0:T(1,128)} %hub_in.1, ...), custom_call_target="tpu_custom_call" | custom-call | tf_op jit(solution)/shard_map/layer/pallas_call | solution.py:500
  60.1 0.8 %finish.1 = (bf16[64,4096]{1,0:T(8,128)(2,1)}, f32[64,128]{1,0:T(8,128)}, f32[64,128]{1,0:T(8,128)}, f32[1,64]{1,0:T(1,128)}) custom-call(bf16[64,4096]{1,0:T(8,128)(2,1)S(1)} %get-tuple-element.10.hidden_ref, f32[64,384]{1,0:T(8,128)S(1)} %get-tuple-element.11.grads_ref), custom_call_target="tpu_custom_call" | custom-call | tf_op jit(solution)/shard_map/finish/pallas_call | solution.py:551

commit v5 on v4

--- a/solution.py
+++ b/solution.py
@@ -9,7 +9,7 @@
 NX, NZ, NN, NF = 4, 8, 64, 4
 TILES = 352
 BLOCKS = 32
-UNROLL = 32
+UNROLL = 88
 FLIPS = 16
 FAR_FIRST = (4, 3, 5, 2, 6, 1, 7)
 PARTS = 8

time: 61 us -> 60.6 us (level)
  no operation moved by 1% of the time
where the time goes in v5:
time: 60.6 us; the launch traced here: 60.5 us
  Pallas kernels  59.2 us (98%)
  between operations  1.29 us (2%)
    pallas_call x1, Pallas kernels, local(): pl.pallas_call(layer_kernel, name='layer', out_shape=(jax.ShapeDtypeStruc...  58.4 us

profile of v5, /device:TPU:1, one launch (start us, length us, event | category | flops | bytes accessed | tf_op | source)
XLA Modules:
  0.0 60.5 jit_solution(17655624268874871498)
XLA Ops:
  1.3 58.4 %layer.1 = (bf16[64,4096]{1,0:T(8,128)(2,1)S(1)}, f32[64,384]{1,0:T(8,128)S(1)}) custom-call(bf16[32,4096]{1,0:T(8,128)(2,1)} %feat_in.1, bf16[128,256]{1,0:T(8,128)(2,1)} %wself_in.1, bf16[128,256]{1,0:T(8,128)(2,1)} %wneigh_in.1, f32[1,256]{1,0:T(1,128)} %bitcast.6, bf16[64,4096]{1,0:T(8,128)(2,1)} %cot_in.1, s32[1,32]{1,0:T(1,128)} %hub_in.1, ...), custom_call_target="tpu_custom_call" | custom-call | tf_op jit(solution)/shard_map/layer/pallas_call | solution.py:500
  59.7 0.8 %finish.1 = (bf16[64,4096]{1,0:T(8,128)(2,1)}, f32[64,128]{1,0:T(8,128)}, f32[64,128]{1,0:T(8,128)}, f32[1,64]{1,0:T(1,128)}) custom-call(bf16[64,4096]{1,0:T(8,128)(2,1)S(1)} %get-tuple-element.10.hidden_ref, f32[64,384]{1,0:T(8,128)S(1)} %get-tuple-element.11.grads_ref), custom_call_target="tpu_custom_call" | custom-call | tf_op jit(solution)/shard_map/finish/pallas_call | solution.py:551

commit v6 on v5

--- a/solution.py
+++ b/solution.py
@@ -54,7 +54,7 @@
     z = (me // 2) % NZ
     x = me // (2 * NZ)
     loads = [
-        started(pltpu.make_async_copy(src, dst, load_sem.at[i]))
+        pltpu.make_async_copy(src, dst, load_sem.at[i])
         for i, (src, dst) in enumerate(
             (
                 (feat_in, feat_ref), (rows_in, rows_ref), (hub_in, hub_ref), (count_in, count_ref),
@@ -64,15 +64,41 @@
             )
         )
     ]
+    for copy in loads[:4]:
+        copy.start()
+    def chip_at(k, dz):
+        dx = 2 + (1 - 2 * (k % 2)) * ((k + 1) // 2)
+        return ((x + dx) % NX) * NZ + (z + dz) % NZ
+
+    def between_chips(i):
+        return [
+            chip_at(2 * (i % 2) + j // 2, 4 + (2 * (j % 2) - 1) * (1 + i // 2)) for j in range(4)
+        ]
+
+    opposite = [chip_at(k, 4) for k in range(4)]
+    level = [chip_at(k, 0) for k in range(3)] + [me // 2]
+    sibling = me + 1 - 2 * core
     barrier = pltpu.get_barrier_semaphore()
 
-    def node_signal(k, _):
-        peer_signal(barrier, (me + k) % NN, feat)
-        return 0
-
-    lax.fori_loop(1, NN, node_signal, 0)
+    def greet(chip):
+        peer_signal(barrier, 2 * chip, feat)
+        peer_signal(barrier, 2 * chip + 1, feat)
+
+    def between_greet(i, _):
+        for chip in between_chips(i):
+            greet(chip)
+        return 0
+
+    for chip in opposite:
+        greet(chip)
+    lax.fori_loop(0, 6, between_greet, 0)
     for k in range(1, NF):
         peer_signal(barrier, me, (feat + k) % NF)
+    for chip in level[:3]:
+        greet(chip)
+    peer_signal(barrier, sibling, feat)
+    for copy in loads[4:]:
+        copy.start()
 
     for copy in loads[:4]:
         copy.wait()
@@ -110,18 +136,9 @@
             outbox.at[node], src_ref.at[32 + me], halo_send.at[node], halo_recv.at[me], node, feat
         )
 
-    def chip_at(k, dz):
-        dx = 2 + (1 - 2 * (k % 2)) * ((k + 1) // 2)
-        return ((x + dx) % NX) * NZ + (z + dz) % NZ
-
     def send(chip):
         halo_copy(2 * chip).start()
         halo_copy(2 * chip + 1).start()
-
-    def between_chips(i):
-        return [
-            chip_at(2 * (i % 2) + j // 2, 4 + (2 * (j % 2) - 1) * (1 + i // 2)) for j in range(4)
-        ]
 
     def between(i, _):
         chips = between_chips(i)
@@ -130,13 +147,11 @@
             send(chip)
         return 0
 
-    sibling = me + 1 - 2 * core
     hubs = jnp.concatenate([hub_ref[...]] * 4, axis=1)
     hubs = jnp.where(lane // 32 % 2 == core, hubs, -1)
     own_hubs = pick([jnp.concatenate([hubs, jnp.full_like(hubs, -1)], axis=1)])[0][:, :128]
     hub0[...] = jnp.where(lane < 64, own_hubs[:16], own_hubs[16:])
     src_ref[32 + me] = jnp.zeros((32, 128), BF16)
-    opposite = [chip_at(k, 4) for k in range(4)]
     fill(opposite)
     pl.semaphore_wait(barrier, NN - 1 + NF - 1)
 
@@ -165,7 +180,6 @@
     for k in FAR_FIRST:
         chip_hubs(k, z).start()
     lax.fori_loop(1, 6, between, 0)
-    level = [chip_at(k, 0) for k in range(3)] + [me // 2]
     fill(level)
     for chip in level[:3]:
         send(chip)

time: 60.6 us -> 60.4 us (level)
  no operation moved by 1% of the time
where the time goes in v6:
time: 60.4 us; the launch traced here: 60.3 us
  Pallas kernels  59 us (98%)
  between operations  1.29 us (2%)
    pallas_call x1, Pallas kernels, local(): pl.pallas_call(layer_kernel, name='layer', out_shape=(jax.ShapeDtypeStruc...  58.2 us

profile of v6, /device:TPU:1, one launch (start us, length us, event | category | flops | bytes accessed | tf_op | source)
XLA Modules:
  0.0 60.3 jit_solution(13233721139617537740)
XLA Ops:
  1.3 58.2 %layer.1 = (bf16[64,4096]{1,0:T(8,128)(2,1)S(1)}, f32[64,384]{1,0:T(8,128)S(1)}) custom-call(bf16[32,4096]{1,0:T(8,128)(2,1)} %feat_in.1, bf16[128,256]{1,0:T(8,128)(2,1)} %wself_in.1, bf16[128,256]{1,0:T(8,128)(2,1)} %wneigh_in.1, f32[1,256]{1,0:T(1,128)} %bitcast.6, bf16[64,4096]{1,0:T(8,128)(2,1)} %cot_in.1, s32[1,32]{1,0:T(1,128)} %hub_in.1, ...), custom_call_target="tpu_custom_call" | custom-call | tf_op jit(solution)/shard_map/layer/pallas_call | solution.py:514
  59.5 0.8 %finish.1 = (bf16[64,4096]{1,0:T(8,128)(2,1)}, f32[64,128]{1,0:T(8,128)}, f32[64,128]{1,0:T(8,128)}, f32[1,64]{1,0:T(1,128)}) custom-call(bf16[64,4096]{1,0:T(8,128)(2,1)S(1)} %get-tuple-element.10.hidden_ref, f32[64,384]{1,0:T(8,128)S(1)} %get-tuple-element.11.grads_ref), custom_call_target="tpu_custom_call" | custom-call | tf_op jit(solution)/shard_map/finish/pallas_call | solution.py:565
